TPU v7x, 256 devices: a whole 4x4x8 slice. The times are simulated.
256 devices in a mesh: gz: 4 (over z_lo), angle: 64 (over z_hi, y, x, core).
Axes of the slice: x: 4, y: 4, z: 8 (z_hi: 2, z_lo: 4; z = z_hi * 4 + z_lo), core: 2. Of those that a mesh axis runs over, the one named last changes fastest.
Arguments:
- index: float32 [4, 256, 256], P('gz'), may hold values from 0 to 0.5
- prop_phase: float32 [256, 256], replicated, may hold values from -3.140625 to 3.140625
- entry_field: float32 [4, 256, 2, 256, 256], P('gz', 'angle'), may hold values from -6 to 6
- exit_cotangent: float32 [256, 2, 256, 256], P('angle'), may hold values from -6 to 6
Outputs:
- new_index: float32 [4, 256, 256], P('gz')
All inputs are finite; a program needn't handle non-finite values.
Results may differ from a plain program's by a relative error of at most 0.0001.
Values sent between devices are 32-bit elements; how exact they have to be, the bound alone decides.
No kernel may reach another device: no remote copies, remote signals or barrier semaphores. Data moves between devices by JAX's collectives and lax.ppermute only.
A program may use at most 128 MiB of HBM per device.

v0:
```python
import math

import jax
import jax.numpy as jnp
from jax import lax
from jax.sharding import PartitionSpec as P

PHASE_GAIN = 2.0
UPDATE_RATE = 4.0


def shifted(x, axis, by):
    devices = lax.axis_size(axis)
    pairs = [(i, i + by) for i in range(devices) if 0 <= i + by < devices]
    return lax.ppermute(x, axis, pairs)


def matmul(matrix, operand):
    return jnp.dot(
        matrix, operand, precision=lax.Precision.HIGHEST, preferred_element_type=jnp.float32
    )


def tables(grid_len):
    indices = jnp.arange(grid_len, dtype=jnp.int32)
    products = indices[:, None] * indices[None, :] % grid_len
    turned = 2.0 * math.pi / grid_len * products.astype(jnp.float32)
    norm_scale = 1.0 / math.sqrt(grid_len)
    return (jnp.cos(turned) * norm_scale, -jnp.sin(turned) * norm_scale)


def left_apply(mat_real, mat_imag, vec_real, vec_imag):
    return (
        matmul(mat_real, vec_real) - matmul(mat_imag, vec_imag),
        matmul(mat_real, vec_imag) + matmul(mat_imag, vec_real),
    )


def right_apply(vec_real, vec_imag, mat_real, mat_imag):
    return (
        matmul(vec_real, mat_real) - matmul(vec_imag, mat_imag),
        matmul(vec_real, mat_imag) + matmul(vec_imag, mat_real),
    )


def propagate(field_real, field_imag, tabs):
    w_real, w_imag, h_real, h_imag = tabs
    h_imag = -h_imag
    spec_real, spec_imag = left_apply(w_real, w_imag, field_real, field_imag)
    spec_real, spec_imag = right_apply(spec_real, spec_imag, w_real, w_imag)
    moved_real = h_real * spec_real - h_imag * spec_imag
    moved_imag = h_real * spec_imag + h_imag * spec_real
    moved_real, moved_imag = left_apply(w_real, -w_imag, moved_real, moved_imag)
    return right_apply(moved_real, moved_imag, w_real, -w_imag)


def forward_slab(entry_now, phase_cos, phase_sin):
    field_real, field_imag = (entry_now[0], entry_now[1])
    kept_real = phase_cos[0] * field_real - phase_sin[0] * field_imag
    kept_imag = phase_cos[0] * field_imag + phase_sin[0] * field_real
    kept_fields = [jnp.stack([kept_real, kept_imag])]
    return jnp.stack(kept_fields)


def adjoint_slab(dual_in, kept_fields, phase_cos, phase_sin, tabs):
    dual_real, dual_imag = (dual_in[0], dual_in[1])
    layer_count = phase_cos.shape[0]
    grad_terms = [None] * layer_count
    back_real, back_imag = propagate(dual_real, dual_imag, tabs)
    kept_real = kept_fields[0, 0]
    kept_imag = kept_fields[0, 1]
    grad_terms[0] = PHASE_GAIN * (back_imag * kept_real - back_real * kept_imag)
    dual_real = phase_cos[0] * back_real + phase_sin[0] * back_imag
    dual_imag = phase_cos[0] * back_imag - phase_sin[0] * back_real
    return (jnp.stack([dual_real, dual_imag]), jnp.stack(grad_terms))


def per_device(index, prop_phase, entry_field, exit_cotangent):
    grid_len = index.shape[1]
    angle_local = entry_field.shape[1]
    w_real, w_imag = tables(grid_len)
    tabs = (w_real, w_imag, jnp.cos(prop_phase), jnp.sin(prop_phase))
    depth_rank = lax.axis_index("gz")
    depth_count = lax.axis_size("gz")
    angle_count = lax.axis_size("angle")
    phase_cos = jnp.cos(PHASE_GAIN * index)
    phase_sin = jnp.sin(PHASE_GAIN * index)

    def kept_for(angle_no):
        entry = lax.dynamic_index_in_dim(entry_field[0], angle_no, 0, keepdims=False)
        return forward_slab(entry, phase_cos, phase_sin)

    grad_terms = jnp.zeros(index.shape, jnp.float32)

    def one_turn(grad_now, item):
        dual_out, terms = adjoint_slab(item[0], kept_for(item[1]), phase_cos, phase_sin, tabs)
        return (grad_now + terms, dual_out)

    def advance(pair_in):
        grad_next, duals_out = lax.scan(
            one_turn, pair_in[1], (pair_in[0], jnp.arange(angle_local, dtype=jnp.int32))
        )
        return (duals_out, grad_next)

    def keep_pair(pair_in):
        return pair_in

    duals = exit_cotangent
    for section_no in range(depth_count - 1, -1, -1):
        duals, grad_terms = lax.cond(
            depth_rank == section_no, advance, keep_pair, (duals, grad_terms)
        )
        if section_no > 0:
            duals = shifted(duals, "gz", -1)
    total_angles = angle_count * angle_local
    grad_total = lax.psum(grad_terms, "angle")
    return jnp.maximum(index - UPDATE_RATE * (grad_total / total_angles), 0.0)


def solution(mesh):
    return jax.shard_map(
        per_device,
        mesh=mesh,
        in_specs=(
            P("gz", None, None),
            P(),
            P("gz", "angle", None, None, None),
            P("angle", None, None, None),
        ),
        out_specs=P("gz", None, None),
        check_vma=False,
    )
```

profile of v0, /device:TPU:1, one launch (start us, length us, event | category | flops | bytes accessed | tf_op | source)
XLA Modules:
  0.0 1241.7 jit_solution(4394889619376874574)
XLA Ops:
  6.5 3.1 copy.57
  9.7 1.1 cosine_multiply_fusion
  10.7 1.0 multiply_sine_fusion
  11.7 1.6 fusion.69
  13.3 1.0 conditional.4
  13.3 0.7 broadcast.39
  14.3 1.3 collective-permute-start
  15.6 46.8 %collective-permute-done = f32[4,2,256,256]{3,2,1,0:T(8,128)} collective-permute-done((f32[4,2,256,256]{3,2,1,0:T(8,128)}, f32[4,2,256,256]{3,2,1,0:T(8,128)}, u32[]{:S(2)}, u32[]{:S(2)}) %collective-permute-start) | collective-permute-done | bytes 2097184 | tf_op jit(solution)/shard_map/ppermute | solution.py:15
  63.0 1.3 collective-permute-start.1
  64.3 48.9 %collective-permute-done.1 = f32[4,2,256,256]{3,2,1,0:T(8,128)} collective-permute-done((f32[4,2,256,256]{3,2,1,0:T(8,128)}, f32[4,2,256,256]{3,2,1,0:T(8,128)}, u32[]{:S(2)}, u32[]{:S(2)}) %collective-permute-start.1) | collective-permute-done | bytes 2097184 | tf_op jit(solution)/shard_map/ppermute | solution.py:15
  113.3 1.3 collective-permute-start.2
  114.6 303.4 %collective-permute-done.2 = f32[4,2,256,256]{3,2,1,0:T(8,128)} collective-permute-done((f32[4,2,256,256]{3,2,1,0:T(8,128)}, f32[4,2,256,256]{3,2,1,0:T(8,128)}, u32[]{:S(2)}, u32[]{:S(2)}) %collective-permute-start.2) | collective-permute-done | bytes 2097184 | tf_op jit(solution)/shard_map/ppermute | solution.py:15
  418.0 76.7 %conditional.7 = (f32[1,256,256]{2,1,0:T(8,128)}) conditional(s32[]{:T(128)} %convert_element_type.141, f32[1,256,256]{2,1,0:T(8,128)} %get-tuple-element.975, (f32[256,256]{1,0:T(8,128)}, f32[256,256]{1,0:T(8,128)S(1)}, f32[256,256]{1,0:T(8,128)S(1)}, f32[256,256]{1,0:T(8,128)S(1)}, f32[256,256]{1,0:T(8,128)S(1)}, ...), branch_computations={%region_12.13_spmd, %region_13.16_spmd} | conditional | flops 3223322624 | bytes 22022736 | solution.py:110
  418.2 1.0 neg.54
  419.3 75.4 %while.54 = (s32[]{:T(128)}, f32[1,256,256]{2,1,0:T(8,128)}, f32[4,2,256,256]{3,2,1,0:T(8,128)}, f32[256,256]{1,0:T(8,128)S(1)}, f32[256,256]{1,0:T(8,128)S(1)},...) while((s32[]{:T(128)}, f32[1,256,256]{2,1,0:T(8,128)}, ...), condition=%wide.region_15.15_spmd, body=%wide.region_14.14_spmd.sunk | while | flops 3222994944 | bytes 19401032 | solution.py:100
  419.3 1.5 fusion.389
  420.9 1.5 convolution_subtract_fusion.24
  422.5 0.6 fusion.390
  423.1 1.5 fusion.391
  424.6 1.5 convolution_add_fusion.31
  427.4 0.6 multiply_add_fusion.12
  428.6 0.6 convolution_add_fusion.33
  429.8 0.6 convolution_subtract_fusion.25
  431.1 0.6 dynamic_slice.62
  433.6 1.1 multiply_subtract_fusion.12
  435.9 2.3 fusion.398
  438.2 1.5 fusion.389
  439.7 1.5 convolution_subtract_fusion.24
  441.9 1.5 fusion.391
  443.5 1.5 convolution_add_fusion.31
  445.0 0.6 convolution_add_fusion.32
  446.2 0.6 multiply_add_fusion.12
  447.5 0.6 convolution_add_fusion.33
  448.7 0.6 convolution_subtract_fusion.25
  449.9 0.6 dynamic_slice.62
  452.4 1.1 multiply_subtract_fusion.12
  453.6 0.6 fusion.396
  454.8 2.3 fusion.398
  457.0 1.5 fusion.389
  458.6 1.5 convolution_subtract_fusion.24
  460.8 1.5 fusion.391
  462.3 1.5 convolution_add_fusion.31
  463.9 0.6 convolution_add_fusion.32
  465.1 0.6 multiply_add_fusion.12
  466.3 0.6 convolution_add_fusion.33
  467.5 0.6 convolution_subtract_fusion.25
  468.7 0.6 dynamic_slice.62
  471.3 1.1 multiply_subtract_fusion.12
  472.4 0.6 fusion.396
  473.6 2.3 fusion.398
  475.9 1.5 fusion.389
  477.4 1.5 convolution_subtract_fusion.24
  479.6 1.5 fusion.391
  481.2 1.5 convolution_add_fusion.31
  482.7 0.6 convolution_add_fusion.32
  483.9 0.6 multiply_add_fusion.12
  485.2 0.6 convolution_add_fusion.33
  486.4 0.6 convolution_subtract_fusion.25
  487.6 0.6 dynamic_slice.62
  490.1 1.1 multiply_subtract_fusion.12
  491.3 0.6 fusion.396
  492.5 2.3 fusion.398
  494.8 738.1 %all-reduce.2.cloned.1.call-done = f32[1,256,256]{2,1,0:T(8,128)} async-done(((f32[1,256,256]{2,1,0:T(8,128)}), f32[1,256,256]{2,1,0:T(8,128)}) %all-reduce.2.cloned.1.call-update) | async-done | bytes 262160 | tf_op jit(solution)/shard_map/psum | solution.py:116
  1232.9 1.8 subtract_maximum_fusion
  (42 shorter events, 15.9 us)
Async XLA Ops:
  6.5 4.2 copy-start
  6.5 5.2 copy-start.1
  6.5 1226.3 %all-reduce.2.cloned.1.call-start = ((), (), s32[]{:S(2)}) async-start(), calls=%async_computation | async-start | bytes 524288 | tf_op jit(solution)/shard_map/psum | solution.py:116
  14.3 48.1 %collective-permute-start = (f32[4,2,256,256]{3,2,1,0:T(8,128)}, f32[4,2,256,256]{3,2,1,0:T(8,128)}, u32[]{:S(2)}, u32[]{:S(2)}) collective-permute-start(f32[4,2,256,256]{3,2,1,0:T(8,128)} %get-tuple-element.971), channel_id=1, source_target_pairs={{64,0},{128,64},{192,128},{65,1},{129,65},{193,129},{66,2},{130,66... | collective-permute-start | bytes 6291464 | tf_op jit(solution)/shard_map/ppermute | solution.py:15
  63.0 50.2 %collective-permute-start.1 = (f32[4,2,256,256]{3,2,1,0:T(8,128)}, f32[4,2,256,256]{3,2,1,0:T(8,128)}, u32[]{:S(2)}, u32[]{:S(2)}) collective-permute-start(f32[4,2,256,256]{3,2,1,0:T(8,128)} %get-tuple-element.973), channel_id=1, source_target_pairs={{64,0},{128,64},{192,128},{65,1},{129,65},{193,129},{66,2},{130,66... | collective-permute-start | bytes 6291464 | tf_op jit(solution)/shard_map/ppermute | solution.py:15
  113.3 304.7 %collective-permute-start.2 = (f32[4,2,256,256]{3,2,1,0:T(8,128)}, f32[4,2,256,256]{3,2,1,0:T(8,128)}, u32[]{:S(2)}, u32[]{:S(2)}) collective-permute-start(f32[4,2,256,256]{3,2,1,0:T(8,128)} %get-tuple-element.976), channel_id=1, source_target_pairs={{64,0},{128,64},{192,128},{65,1},{129,65},{193,129},{66,2},{130,66... | collective-permute-start | bytes 6291464 | tf_op jit(solution)/shard_map/ppermute | solution.py:15
Sparse Core Ops, SparseCore 0:
  494.9 737.9 all-reduce.1
where the time goes:
time: 1250 us; the launch traced here: 1240 us
  waiting for transfers between devices  1140 us (91%)
  matrix products  60.2 us (5%)
  between operations  13.7 us (1%)
    psum x1, waiting for transfers between devices, per_device(): grad_total = lax.psum(grad_terms, 'angle')  738 us
    ppermute x3, waiting for transfers between devices, shifted(): return lax.ppermute(x, axis, pairs)  399 us
    dot_general x64, matrix products, matmul(): jnp.dot(matrix, operand, precision=lax.Precision.HIGHEST, preferred_eleme...  60.2 us
  transfers between devices with their start and end apart: 4, of which 4 were waited for; matrix products, arithmetic and copies ran while one was open for 0% of the time, Pallas kernels for 0%

commit v1 on v0

v1 whole, which is shorter than its diff:
```python
import jax
import jax.numpy as jnp
import ml_dtypes
import numpy as np
from jax import lax
from jax.experimental import pallas as pl
from jax.experimental.pallas import tpu as pltpu
from jax.sharding import PartitionSpec as P

PHASE_GAIN = 2.0
UPDATE_RATE = 4.0
VMEM_BYTES = 56 * 2**20


def two_terms(matrix):
    matrix = matrix.astype(np.float32)
    high = matrix.astype(ml_dtypes.bfloat16)
    low = (matrix - high.astype(np.float32)).astype(ml_dtypes.bfloat16)
    return high, low, np.zeros_like(low)


def transform_tables(grid_len):
    quarter = grid_len // 4
    j = np.arange(quarter)
    left_fwd, right_fwd, right_inv, left_inv = [], [], [], []

    def as_real(matrix):
        return np.block([[matrix.real, -matrix.imag], [matrix.imag, matrix.real]])

    def on_left(matrix):
        high, low, zero = two_terms(matrix)
        return np.block([[high, high], [low, zero]])

    def on_right(matrix):
        high, low, zero = two_terms(matrix)
        return np.block([[high, low], [high, zero]])

    for residue in range(4):
        turns = (residue * j[None, :]) / grid_len + (j[:, None] * j[None, :] % quarter) / quarter
        fwd = np.exp(-2j * np.pi * turns) / np.sqrt(grid_len)
        inv = np.conj(fwd).T
        flip = np.where(j.repeat(2) < 0, 0.0, 1.0)
        flip[quarter:] = -1.0 if residue in (1, 2) else 1.0
        left_fwd.append(on_left(as_real(fwd)))
        right_fwd.append(on_right(as_real(fwd).T * flip[:, None]))
        right_inv.append(on_right(as_real(inv).T * flip[None, :]))
        left_inv.append(on_left(as_real(inv)))
    return np.stack([np.stack(m) for m in (left_fwd, right_fwd, right_inv, left_inv)])


def split(block):
    high = block.astype(jnp.bfloat16)
    return high, (block - high.astype(jnp.float32)).astype(jnp.bfloat16)


def left_mul(matrix, block):
    both = jnp.dot(
        matrix, jnp.concatenate(split(block), 0), preferred_element_type=jnp.float32
    )
    return both[:128] + both[128:]


def right_mul(block, matrix):
    both = jnp.dot(
        jnp.concatenate(split(block), 1), matrix, preferred_element_type=jnp.float32
    )
    return both[:, :128] + both[:, 128:]


def half_turn(block):
    return pltpu.roll(block, 64, 1)


def adjoint_step(loads, stores, tabs, h_same, h_cross):
    count = len(loads)
    low = lax.broadcasted_iota(jnp.int32, (256 * count, 128), 1) < 64
    sign = jnp.where(low, -1.0, 1.0)

    def rows(a, b):
        return jnp.concatenate([a, b], 0)

    reals, imags = [], []
    for load in loads:
        (x0r, x0i), (x1r, x1i), (x2r, x2i), (x3r, x3i) = [load(p) for p in range(4)]
        s0r, s0i, s1r, s1i = x0r + x2r, x0i + x2i, x1r + x3r, x1i + x3i
        d0r, d0i, d1r, d1i = x0r - x2r, x0i - x2i, x1r - x3r, x1i - x3i
        parts = (
            rows(s0r + s1r, s0i + s1i),
            rows(d0r + d1i, d0i - d1r),
            rows(s0r - s1r, s0i - s1i),
            rows(d0r - d1i, d0i + d1r),
        )
        for p in range(4):
            out = left_mul(tabs[0, p], parts[p])
            reals.append(out[:64])
            imags.append(out[64:])
    yr, yi = jnp.concatenate(reals, 0), jnp.concatenate(imags, 0)

    sr, si = yr[:, :128] + yr[:, 128:], yi[:, :128] + yi[:, 128:]
    dr, di = yr[:, :128] - yr[:, 128:], yi[:, :128] - yi[:, 128:]
    t = jnp.where(low, sr, si)
    u = half_turn(jnp.where(low, si, sr))
    v = half_turn(di)
    a, b = dr + v, dr - v
    parts = (t + u, jnp.where(low, a, b), t - u, jnp.where(low, b, a))
    back = []
    for k in range(4):
        z = right_mul(parts[k], tabs[1, k])
        w = half_turn(z)
        z = jnp.concatenate(
            [
                z[256 * n : 256 * n + 256] * h_same[k] + w[256 * n : 256 * n + 256] * h_cross[k]
                for n in range(count)
            ],
            0,
        )
        back.append(right_mul(z, tabs[2, k]))

    t = back[0] + back[2]
    u = half_turn(back[0] - back[2])
    er, ei = jnp.where(low, t, u), jnp.where(low, u, t)
    fr, fi = back[1] + back[3], half_turn(back[1] - back[3]) * sign
    xr = jnp.concatenate([er + fr, er - fr], 1)
    xi = jnp.concatenate([ei + fi, ei - fi], 1)
    for n in range(count):
        c = []
        for p in range(4):
            at = 256 * n + 64 * p
            out = left_mul(tabs[3, p], rows(xr[at : at + 64], xi[at : at + 64]))
            c.append((out[:64], out[64:]))
        (c0r, c0i), (c1r, c1i), (c2r, c2i), (c3r, c3i) = c
        e0r, e0i, e1r, e1i = c0r + c2r, c0i + c2i, c0r - c2r, c0i - c2i
        f0r, f0i, f1r, f1i = c1r + c3r, c1i + c3i, c3i - c1i, c1r - c3r
        stores[n](0, e0r + f0r, e0i + f0i)
        stores[n](1, e1r + f1r, e1i + f1i)
        stores[n](2, e0r - f0r, e0i - f0i)
        stores[n](3, e1r - f1r, e1i - f1i)


def quarter_at(p):
    return pl.ds(64 * p, 64)


def store_into(ref, angle):
    def store(p, real, imag):
        ref[angle, 0, quarter_at(p), :] = real
        ref[angle, 1, quarter_at(p), :] = imag

    return store


def half_range_cos_sin(turn):
    sq = turn * turn
    c = 1.0 / 479001600.0
    for n in (-1.0 / 3628800.0, 1.0 / 40320.0, -1.0 / 720.0, 1.0 / 24.0, -0.5, 1.0):
        c = c * sq + n
    s = -1.0 / 39916800.0
    for n in (1.0 / 362880.0, -1.0 / 5040.0, 1.0 / 120.0, -1.0 / 6.0, 1.0):
        s = s * sq + n
    return c, s * turn


def first_kernel(dual, phase, tabs, mu, h_same, h_cross, lanes):
    row = lax.broadcasted_iota(jnp.int32, (256, 128), 0)
    lane = lax.broadcasted_iota(jnp.int32, (256, 128), 1)
    col = lane % 64 * 4
    sign = jnp.where(lane < 64, 1.0, -1.0)
    for n in range(2):
        lanes[pl.ds(256 * n, 256), :] = phase[:, pl.ds(128 * n, 128)]
    turn = jnp.concatenate(
        [
            jnp.concatenate([lanes[pl.ds(256 * n + q, 64, stride=4), :] for q in range(4)], 0)
            for n in range(2)
        ],
        1,
    )
    c, s = half_range_cos_sin(0.5 * turn)
    hr, hi = split(1.0 - 2.0 * s * s), split(2.0 * s * c)
    for k in range(4):
        pick = jnp.where(row == col + k, 1.0, 0.0).astype(jnp.bfloat16)
        same, cross = [
            sum(jnp.dot(term, pick, preferred_element_type=jnp.float32) for term in h)
            for h in (hr, hi)
        ]
        h_same[k] = same
        h_cross[k] = cross * sign

    def load_from(angle):
        return lambda p: (dual[angle, 0, quarter_at(p), :], dual[angle, 1, quarter_at(p), :])

    count = dual.shape[0]
    adjoint_step(
        [load_from(n) for n in range(count)],
        [store_into(mu, n) for n in range(count)],
        tabs,
        h_same,
        h_cross,
    )


def rest_kernel(mu_in, h_same, h_cross, tabs, entry, own, near, mid, far, keep, send, mu, tr, ti):
    count = mu_in.shape[0]
    mu[...] = mu_in[...]
    left = 3 - lax.axis_index("gz")

    def set_t(ref):
        c, s = half_range_cos_sin(PHASE_GAIN * ref[...])
        tr[...] = c
        ti[...] = s

    def load_from(angle):
        def load(p):
            at = quarter_at(p)
            r, i = mu[angle, 0, at, :], mu[angle, 1, at, :]
            return tr[at, :] * r + ti[at, :] * i, tr[at, :] * i - ti[at, :] * r

        return load

    def one_slab(step, carry):
        ahead = left - step
        for distance, ref in ((3, far), (2, mid), (1, near)):
            pl.when(ahead == distance)(lambda ref=ref: set_t(ref))
        adjoint_step(
            [load_from(n) for n in range(count)],
            [store_into(mu, n) for n in range(count)],
            tabs,
            h_same,
            h_cross,
        )
        return carry

    lax.fori_loop(0, left, one_slab, 0)
    set_t(own)
    other = 1 - lax.axis_index("angle") % 2

    def terms(at):
        gr = gi = 0.0
        for n in range(count):
            r, i = mu[n, 0, at, :], mu[n, 1, at, :]
            er, ei = entry[n, 0, at, :], entry[n, 1, at, :]
            gr += r * er + i * ei
            gi += i * er - r * ei
        return PHASE_GAIN * (tr[at, :] * gi - ti[at, :] * gr)

    for at in range(0, 128, 32):
        keep[pl.ds(at, 32), :] = terms(pl.ds(pl.multiple_of(128 - 128 * other + at, 32), 32))
        send[pl.ds(at, 32), :] = terms(pl.ds(pl.multiple_of(128 * other + at, 32), 32))


def call(kernel, out_shape, scratch=()):
    return pl.pallas_call(
        kernel,
        out_shape=out_shape,
        scratch_shapes=list(scratch),
        compiler_params=pltpu.CompilerParams(vmem_limit_bytes=VMEM_BYTES),
    )


def f32(*shape):
    return jax.ShapeDtypeStruct(shape, jnp.float32)


def angle_pairs(partner):
    pairs = []
    for n in range(64):
        z, y, x, c = partner(n // 32, n // 8 % 4, n // 2 % 4, n % 2)
        pairs.append((n, z * 32 + y * 8 + x * 2 + c))
    return pairs


def per_device(index, prop_phase, entry_field, exit_cotangent):
    count = exit_cotangent.shape[0]
    tabs = jnp.asarray(transform_tables(256))
    own = index[0]
    near, mid, far = [
        lax.ppermute(own, "gz", [(n, n - by) for n in range(by, 4)]) for by in (1, 2, 3)
    ]
    mu, h_same, h_cross = call(
        first_kernel,
        (f32(count, 2, 256, 256), f32(4, 256, 128), f32(4, 256, 128)),
        (pltpu.VMEM((512, 128), jnp.float32),),
    )(exit_cotangent, prop_phase, tabs)
    plane = pltpu.VMEM((256, 256), jnp.float32)
    keep, send = call(
        rest_kernel,
        (f32(128, 256), f32(128, 256)),
        (pltpu.VMEM((count, 2, 256, 256), jnp.float32), plane, plane),
    )(mu, h_same, h_cross, tabs, entry_field[0], own, near, mid, far)

    core = lax.axis_index("angle") % 2
    swap = angle_pairs(lambda z, y, x, c: (z, y, x, 1 - c))
    total = keep + lax.ppermute(send, "angle", swap)
    for partner in (
        lambda z, y, x, c: (z, y, x ^ 1, c),
        lambda z, y, x, c: (z, y, 3 - x, c),
        lambda z, y, x, c: (z, y ^ 1, x, c),
        lambda z, y, x, c: (z, 3 - y, x, c),
        lambda z, y, x, c: (1 - z, y, x, c),
    ):
        total = total + lax.ppermute(total, "angle", angle_pairs(partner))
    angles = count * lax.axis_size("angle")
    mine = lax.dynamic_slice_in_dim(own, core * 128, 128, 0)
    new = jnp.maximum(mine - UPDATE_RATE * (total / angles), 0.0)
    other = lax.ppermute(new, "angle", swap)
    return jnp.where(
        core == 0, jnp.concatenate([new, other], 0), jnp.concatenate([other, new], 0)
    )[None]


def solution(mesh):
    return jax.shard_map(
        per_device,
        mesh=mesh,
        in_specs=(
            P("gz", None, None),
            P(),
            P("gz", "angle", None, None, None),
            P("angle", None, None, None),
        ),
        out_specs=P("gz", None, None),
        check_vma=False,
    )
```

time: 1250 us -> 83.1 us (0.07)
  waiting for transfers between devices: 1140 us -> 34.2 us
  matrix products: 60.2 us -> 0 us
  Pallas kernels: 0 us -> 22.8 us
  starting transfers between devices: 3.88 us -> 23.3 us
  between operations: 13.7 us -> 0.06 us
    psum x1 -> x0, waiting for transfers between devices: 738 us -> none  [per_device(): grad_total = lax.psum(grad_terms, 'angle')]
    ppermute x3 -> x10, waiting for transfers between devices: 399 us -> 34.2 us  [the longest x3 17.3 us: per_device(): lax.ppermute(own, 'gz', [(n, n - by) for n in range(by, 4)])]
    dot_general x64 -> x0, matrix products: 60.2 us -> none  [matmul(): jnp.dot(matrix, operand, precision=lax.Precision.HIGHEST, preferred_eleme...]
    pallas_call x0 -> x2, Pallas kernels: none -> 22.8 us  [the longest x1 15.4 us: per_device(): call(rest_kernel, (f32(128, 256), f32(128, 256)), (pltpu.VMEM((count, 2,...]
    ppermute x3 -> x10, starting transfers between devices: 3.88 us -> 23.3 us  [the longest x5 14 us: per_device(): total = total + lax.ppermute(total, 'angle', angle_pairs(partner))]
  transfers between devices with their start and end apart: 4 -> 10, of which waited for: 4 -> 8; matrix products, arithmetic and copies ran while one was open for 0% -> 0% of each run, Pallas kernels for 0% -> 9%
where the time goes in v1:
time: 83.1 us; the launch traced here: 83 us
  waiting for transfers between devices  34.2 us (41%)
  starting transfers between devices  23.3 us (28%)
  Pallas kernels  22.8 us (27%)
  other arithmetic  1.74 us (2%)
    ppermute x3, waiting for transfers between devices, per_device(): lax.ppermute(own, 'gz', [(n, n - by) for n in range(by, 4)])  17.3 us
    pallas_call x1, Pallas kernels, per_device(): call(rest_kernel, (f32(128, 256), f32(128, 256)), (pltpu.VMEM((count, 2,...  15.4 us
    ppermute x5, waiting for transfers between devices, per_device(): total = total + lax.ppermute(total, 'angle', angle_pairs(partner))  14.7 us
    ppermute x5, starting transfers between devices, per_device(): total = total + lax.ppermute(total, 'angle', angle_pairs(partner))  14 us
    pallas_call x1, Pallas kernels, per_device(): call(first_kernel, (f32(count, 2, 256, 256), f32(4, 256, 128), f32(4, 256...  7.46 us
    ppermute x1, starting transfers between devices, per_device(): other = lax.ppermute(new, 'angle', swap)  4.12 us
    ppermute x3, starting transfers between devices, per_device(): lax.ppermute(own, 'gz', [(n, n - by) for n in range(by, 4)])  3.86 us
  transfers between devices with their start and end apart: 10, of which 8 were waited for; matrix products, arithmetic and copies ran while one was open for 0% of the time, Pallas kernels for 9%

profile of v1, /device:TPU:1, one launch (start us, length us, event | category | flops | bytes accessed | tf_op | source)
XLA Modules:
  0.0 83.0 jit_solution(17762182603453218130)
XLA Ops:
  0.0 1.3 %collective-permute-start = (f32[256,256]{1,0:T(8,128)}, f32[256,256]{1,0:T(8,128)S(1)}, u32[]{:S(2)}, u32[]{:S(2)}) collective-permute-start(f32[256,256]{1,0:T(8,128)} %bitcast.9), channel_id=1, source_target_pairs={{64,0},{128,64},{192,128},{65,1},{129,65},{193,129},{66,2},{130,66... | collective-permute-start | bytes 786440 | tf_op jit(solution)/shard_map/ppermute | solution.py:276
  1.3 1.3 %collective-permute-start.1 = (f32[256,256]{1,0:T(8,128)}, f32[256,256]{1,0:T(8,128)S(1)}, u32[]{:S(2)}, u32[]{:S(2)}) collective-permute-start(f32[256,256]{1,0:T(8,128)} %bitcast.10), channel_id=1, source_target_pairs={{128,0},{192,64},{129,1},{193,65},{130,2},{194,66},{131,3},{195,67... | collective-permute-start | bytes 786440 | tf_op jit(solution)/shard_map/ppermute | solution.py:276
  2.6 1.3 %collective-permute-start.2 = (f32[256,256]{1,0:T(8,128)}, f32[256,256]{1,0:T(8,128)S(1)}, u32[]{:S(2)}, u32[]{:S(2)}) collective-permute-start(f32[256,256]{1,0:T(8,128)} %bitcast.11), channel_id=1, source_target_pairs={{192,0},{193,1},{194,2},{195,3},{196,4},{197,5},{198,6},{199,7},{2... | collective-permute-start | bytes 786440 | tf_op jit(solution)/shard_map/ppermute | solution.py:276
  3.9 7.5 %shard_map.55 = (f32[4,2,256,256]{3,2,1,0:T(8,128)}, f32[4,256,128]{2,1,0:T(8,128)}, f32[4,256,128]{2,1,0:T(8,128)}) custom-call(f32[4,2,256,256]{3,2,1,0:T(8,128)} %dual.1, f32[256,256]{1,0:T(8,128)} %phase.1, bf16[4,4,256,256]{3,2,1,0:T(8,128)(2,1)} %constant.32.clone.tabs), custom_call_target="tpu_custom_call" | custom-call | tf_op jit(solution)/shard_map/pallas_call | solution.py:278
  11.4 0.0 collective-permute-done.near
  11.4 0.0 copy-start.1
  11.4 17.3 %collective-permute-done.1.mid = f32[256,256]{1,0:T(8,128)S(1)} collective-permute-done((f32[256,256]{1,0:T(8,128)}, f32[256,256]{1,0:T(8,128)S(1)}, u32[]{:S(2)}, u32[]{:S(2)}) %collective-permute-start.1) | collective-permute-done | bytes 262176 | tf_op jit(solution)/shard_map/ppermute | solution.py:276
  28.7 0.0 copy-start.2
  28.7 0.0 collective-permute-done.2.far
  28.7 0.0 copy-start.3
  28.7 0.0 copy-done.1
  28.7 0.7 copy-done.2
  29.4 0.1 copy-done.3
  29.5 0.0 copy-start
  29.5 15.4 %shard_map.56 = (f32[128,256]{1,0:T(8,128)}, f32[128,256]{1,0:T(8,128)}) custom-call(f32[4,2,256,256]{3,2,1,0:T(8,128)} %get-tuple-element.10.mu_in, f32[4,256,128]{2,1,0:T(8,128)} %get-tuple-element.11.h_same, f32[4,256,128]{2,1,0:T(8,128)} %get-tuple-element.12.h_cross, bf16[4,4,256,256]{3,2,1,0:T(8,128)(2,1)} %constant.32.clone.tabs, ...), custom_call_target="tpu_custom_call" | custom-call | tf_op jit(solution)/shard_map/pallas_call | solution.py:284
  44.9 1.3 %collective-permute-start.3 = (f32[128,256]{1,0:T(8,128)}, f32[128,256]{1,0:T(8,128)S(1)}, u32[]{:S(2)}, u32[]{:S(2)}) collective-permute-start(f32[128,256]{1,0:T(8,128)} %get-tuple-element.14), channel_id=1, source_target_pairs={{0,1},{1,0},{2,3},{3,2},{4,5},{5,4},{6,7},{7,6},{8,9},{9,8},{10,11... | collective-permute-start | bytes 393224 | tf_op jit(solution)/shard_map/ppermute | solution.py:292
  46.2 1.2 %collective-permute-done.3 = f32[128,256]{1,0:T(8,128)S(1)} collective-permute-done((f32[128,256]{1,0:T(8,128)}, f32[128,256]{1,0:T(8,128)S(1)}, u32[]{:S(2)}, u32[]{:S(2)}) %collective-permute-start.3) | collective-permute-done | bytes 131104 | tf_op jit(solution)/shard_map/ppermute | solution.py:292
  47.4 0.9 %add.27 = f32[128,256]{1,0:T(8,128)S(1)} add(f32[128,256]{1,0:T(8,128)} %get-tuple-element.13, f32[128,256]{1,0:T(8,128)S(1)} %collective-permute-done.3) | non-fusion elementwise | flops 32768 | bytes 393216 | tf_op jit(solution)/shard_map/add | solution.py:292
  48.4 1.3 %collective-permute-start.4 = (f32[128,256]{1,0:T(8,128)S(1)}, f32[128,256]{1,0:T(8,128)S(1)}, u32[]{:S(2)}, u32[]{:S(2)}) collective-permute-start(f32[128,256]{1,0:T(8,128)S(1)} %add.27), channel_id=1, source_target_pairs={{0,2},{1,3},{2,0},{3,1},{4,6},{5,7},{6,4},{7,5},{8,10},{9,11},{10,... | collective-permute-start | bytes 393224 | tf_op jit(solution)/shard_map/ppermute | solution.py:300
  49.6 3.5 %collective-permute-done.4 = f32[128,256]{1,0:T(8,128)S(1)} collective-permute-done((f32[128,256]{1,0:T(8,128)S(1)}, f32[128,256]{1,0:T(8,128)S(1)}, u32[]{:S(2)}, u32[]{:S(2)}) %collective-permute-start.4) | collective-permute-done | bytes 131104 | tf_op jit(solution)/shard_map/ppermute | solution.py:300
  53.2 2.6 %collective-permute-start.5 = (f32[128,256]{1,0:T(8,128)S(1)}, f32[128,256]{1,0:T(8,128)S(1)}, u32[]{:S(2)}, u32[]{:S(2)}) collective-permute-start(f32[128,256]{1,0:T(8,128)S(1)} %add.28), channel_id=1, source_target_pairs={{0,6},{1,7},{2,4},{3,5},{4,2},{5,3},{6,0},{7,1},{8,14},{9,15},{10,... | collective-permute-start | bytes 393224 | tf_op jit(solution)/shard_map/ppermute | solution.py:300
  55.7 2.6 %collective-permute-done.5 = f32[128,256]{1,0:T(8,128)S(1)} collective-permute-done((f32[128,256]{1,0:T(8,128)S(1)}, f32[128,256]{1,0:T(8,128)S(1)}, u32[]{:S(2)}, u32[]{:S(2)}) %collective-permute-start.5) | collective-permute-done | bytes 131104 | tf_op jit(solution)/shard_map/ppermute | solution.py:300
  58.3 1.4 %collective-permute-start.6 = (f32[128,256]{1,0:T(8,128)S(1)}, f32[128,256]{1,0:T(8,128)S(1)}, u32[]{:S(2)}, u32[]{:S(2)}) collective-permute-start(f32[128,256]{1,0:T(8,128)S(1)} %add.29), channel_id=1, source_target_pairs={{0,8},{1,9},{2,10},{3,11},{4,12},{5,13},{6,14},{7,15},{8,0},{9,1},... | collective-permute-start | bytes 393224 | tf_op jit(solution)/shard_map/ppermute | solution.py:300
  59.7 2.5 %collective-permute-done.6 = f32[128,256]{1,0:T(8,128)S(1)} collective-permute-done((f32[128,256]{1,0:T(8,128)S(1)}, f32[128,256]{1,0:T(8,128)S(1)}, u32[]{:S(2)}, u32[]{:S(2)}) %collective-permute-start.6) | collective-permute-done | bytes 131104 | tf_op jit(solution)/shard_map/ppermute | solution.py:300
  62.2 2.8 %collective-permute-start.7 = (f32[128,256]{1,0:T(8,128)S(1)}, f32[128,256]{1,0:T(8,128)S(1)}, u32[]{:S(2)}, u32[]{:S(2)}) collective-permute-start(f32[128,256]{1,0:T(8,128)S(1)} %add.30), channel_id=1, source_target_pairs={{0,24},{1,25},{2,26},{3,27},{4,28},{5,29},{6,30},{7,31},{8,16},{9,... | collective-permute-start | bytes 393224 | tf_op jit(solution)/shard_map/ppermute | solution.py:300
  65.1 2.4 %collective-permute-done.7 = f32[128,256]{1,0:T(8,128)S(1)} collective-permute-done((f32[128,256]{1,0:T(8,128)S(1)}, f32[128,256]{1,0:T(8,128)S(1)}, u32[]{:S(2)}, u32[]{:S(2)}) %collective-permute-start.7) | collective-permute-done | bytes 131104 | tf_op jit(solution)/shard_map/ppermute | solution.py:300
  67.4 5.9 %collective-permute-start.8 = (f32[128,256]{1,0:T(8,128)S(1)}, f32[128,256]{1,0:T(8,128)S(1)}, u32[]{:S(2)}, u32[]{:S(2)}) collective-permute-start(f32[128,256]{1,0:T(8,128)S(1)} %add.31), channel_id=1, source_target_pairs={{0,32},{1,33},{2,34},{3,35},{4,36},{5,37},{6,38},{7,39},{8,40},{9,... | collective-permute-start | bytes 393224 | tf_op jit(solution)/shard_map/ppermute | solution.py:300
  73.4 3.8 %collective-permute-done.8 = f32[128,256]{1,0:T(8,128)S(1)} collective-permute-done((f32[128,256]{1,0:T(8,128)S(1)}, f32[128,256]{1,0:T(8,128)S(1)}, u32[]{:S(2)}, u32[]{:S(2)}) %collective-permute-start.8) | collective-permute-done | bytes 131104 | tf_op jit(solution)/shard_map/ppermute | solution.py:300
  77.1 0.0 copy-done
  77.2 4.1 %collective-permute-start.9 = (f32[128,256]{1,0:T(8,128)S(1)}, f32[128,256]{1,0:T(8,128)S(1)}, u32[]{:S(2)}, u32[]{:S(2)}) collective-permute-start(f32[128,256]{1,0:T(8,128)S(1)} %fusion), channel_id=1, source_target_pairs={{0,1},{1,0},{2,3},{3,2},{4,5},{5,4},{6,7},{7,6},{8,9},{9,8},{10,11... | collective-permute-start | bytes 393224 | tf_op jit(solution)/shard_map/ppermute | solution.py:304
  81.3 1.0 %collective-permute-done.9 = f32[128,256]{1,0:T(8,128)S(1)} collective-permute-done((f32[128,256]{1,0:T(8,128)S(1)}, f32[128,256]{1,0:T(8,128)S(1)}, u32[]{:S(2)}, u32[]{:S(2)}) %collective-permute-start.9) | collective-permute-done | bytes 131104 | tf_op jit(solution)/shard_map/ppermute | solution.py:304
  82.3 0.7 maximum_select_fusion
  (5 shorter events, 0.1 us)
Async XLA Ops:
  0.0 11.4 %collective-permute-start = (f32[256,256]{1,0:T(8,128)}, f32[256,256]{1,0:T(8,128)S(1)}, u32[]{:S(2)}, u32[]{:S(2)}) collective-permute-start(f32[256,256]{1,0:T(8,128)} %bitcast.9), channel_id=1, source_target_pairs={{64,0},{128,64},{192,128},{65,1},{129,65},{193,129},{66,2},{130,66... | collective-permute-start | bytes 786440 | tf_op jit(solution)/shard_map/ppermute | solution.py:276
  1.3 27.4 %collective-permute-start.1 = (f32[256,256]{1,0:T(8,128)}, f32[256,256]{1,0:T(8,128)S(1)}, u32[]{:S(2)}, u32[]{:S(2)}) collective-permute-start(f32[256,256]{1,0:T(8,128)} %bitcast.10), channel_id=1, source_target_pairs={{128,0},{192,64},{129,1},{193,65},{130,2},{194,66},{131,3},{195,67... | collective-permute-start | bytes 786440 | tf_op jit(solution)/shard_map/ppermute | solution.py:276
  2.6 26.1 %collective-permute-start.2 = (f32[256,256]{1,0:T(8,128)}, f32[256,256]{1,0:T(8,128)S(1)}, u32[]{:S(2)}, u32[]{:S(2)}) collective-permute-start(f32[256,256]{1,0:T(8,128)} %bitcast.11), channel_id=1, source_target_pairs={{192,0},{193,1},{194,2},{195,3},{196,4},{197,5},{198,6},{199,7},{2... | collective-permute-start | bytes 786440 | tf_op jit(solution)/shard_map/ppermute | solution.py:276
  11.4 17.4 %copy-start.1 = (f32[256,256]{1,0:T(8,128)}, f32[256,256]{1,0:T(8,128)S(1)}, u32[]{:S(2)}) copy-start(f32[256,256]{1,0:T(8,128)S(1)} %collective-permute-done.near) | copy-start | bytes 786436
  28.7 0.7 copy-start.2
  28.7 0.8 copy-start.3
  29.5 47.6 %copy-start = (f32[1,256,256]{2,1,0:T(8,128)S(1)}, f32[1,256,256]{2,1,0:T(8,128)}, u32[]{:S(2)}) copy-start(f32[1,256,256]{2,1,0:T(8,128)} %param.5) | copy-start | bytes 786436
  44.9 2.5 %collective-permute-start.3 = (f32[128,256]{1,0:T(8,128)}, f32[128,256]{1,0:T(8,128)S(1)}, u32[]{:S(2)}, u32[]{:S(2)}) collective-permute-start(f32[128,256]{1,0:T(8,128)} %get-tuple-element.14), channel_id=1, source_target_pairs={{0,1},{1,0},{2,3},{3,2},{4,5},{5,4},{6,7},{7,6},{8,9},{9,8},{10,11... | collective-permute-start | bytes 393224 | tf_op jit(solution)/shard_map/ppermute | solution.py:292
  48.4 4.8 %collective-permute-start.4 = (f32[128,256]{1,0:T(8,128)S(1)}, f32[128,256]{1,0:T(8,128)S(1)}, u32[]{:S(2)}, u32[]{:S(2)}) collective-permute-start(f32[128,256]{1,0:T(8,128)S(1)} %add.27), channel_id=1, source_target_pairs={{0,2},{1,3},{2,0},{3,1},{4,6},{5,7},{6,4},{7,5},{8,10},{9,11},{10,... | collective-permute-start | bytes 393224 | tf_op jit(solution)/shard_map/ppermute | solution.py:300
  53.2 5.1 %collective-permute-start.5 = (f32[128,256]{1,0:T(8,128)S(1)}, f32[128,256]{1,0:T(8,128)S(1)}, u32[]{:S(2)}, u32[]{:S(2)}) collective-permute-start(f32[128,256]{1,0:T(8,128)S(1)} %add.28), channel_id=1, source_target_pairs={{0,6},{1,7},{2,4},{3,5},{4,2},{5,3},{6,0},{7,1},{8,14},{9,15},{10,... | collective-permute-start | bytes 393224 | tf_op jit(solution)/shard_map/ppermute | solution.py:300
  58.3 3.9 %collective-permute-start.6 = (f32[128,256]{1,0:T(8,128)S(1)}, f32[128,256]{1,0:T(8,128)S(1)}, u32[]{:S(2)}, u32[]{:S(2)}) collective-permute-start(f32[128,256]{1,0:T(8,128)S(1)} %add.29), channel_id=1, source_target_pairs={{0,8},{1,9},{2,10},{3,11},{4,12},{5,13},{6,14},{7,15},{8,0},{9,1},... | collective-permute-start | bytes 393224 | tf_op jit(solution)/shard_map/ppermute | solution.py:300
  62.2 5.2 %collective-permute-start.7 = (f32[128,256]{1,0:T(8,128)S(1)}, f32[128,256]{1,0:T(8,128)S(1)}, u32[]{:S(2)}, u32[]{:S(2)}) collective-permute-start(f32[128,256]{1,0:T(8,128)S(1)} %add.30), channel_id=1, source_target_pairs={{0,24},{1,25},{2,26},{3,27},{4,28},{5,29},{6,30},{7,31},{8,16},{9,... | collective-permute-start | bytes 393224 | tf_op jit(solution)/shard_map/ppermute | solution.py:300
  67.4 9.7 %collective-permute-start.8 = (f32[128,256]{1,0:T(8,128)S(1)}, f32[128,256]{1,0:T(8,128)S(1)}, u32[]{:S(2)}, u32[]{:S(2)}) collective-permute-start(f32[128,256]{1,0:T(8,128)S(1)} %add.31), channel_id=1, source_target_pairs={{0,32},{1,33},{2,34},{3,35},{4,36},{5,37},{6,38},{7,39},{8,40},{9,... | collective-permute-start | bytes 393224 | tf_op jit(solution)/shard_map/ppermute | solution.py:300
  77.2 5.1 %collective-permute-start.9 = (f32[128,256]{1,0:T(8,128)S(1)}, f32[128,256]{1,0:T(8,128)S(1)}, u32[]{:S(2)}, u32[]{:S(2)}) collective-permute-start(f32[128,256]{1,0:T(8,128)S(1)} %fusion), channel_id=1, source_target_pairs={{0,1},{1,0},{2,3},{3,2},{4,5},{5,4},{6,7},{7,6},{8,9},{9,8},{10,11... | collective-permute-start | bytes 393224 | tf_op jit(solution)/shard_map/ppermute | solution.py:304

commit v2 on v1

--- a/solution.py
+++ b/solution.py
@@ -9,7 +9,7 @@
 
 PHASE_GAIN = 2.0
 UPDATE_RATE = 4.0
-VMEM_BYTES = 56 * 2**20
+VMEM_BYTES = 28 * 2**20
 
 
 def two_terms(matrix):
@@ -160,6 +160,13 @@
     return c, s * turn
 
 
+def start_all(pairs, sems):
+    copies = [pltpu.make_async_copy(a, b, sems.at[n]) for n, (a, b) in enumerate(pairs)]
+    for copy in copies:
+        copy.start()
+    return copies
+
+
 def first_kernel(dual, phase, tabs, mu, h_same, h_cross, lanes):
     row = lax.broadcasted_iota(jnp.int32, (256, 128), 0)
     lane = lax.broadcasted_iota(jnp.int32, (256, 128), 1)
@@ -198,15 +205,30 @@
     )
 
 
-def rest_kernel(mu_in, h_same, h_cross, tabs, entry, own, near, mid, far, keep, send, mu, tr, ti):
-    count = mu_in.shape[0]
-    mu[...] = mu_in[...]
+def rest_kernel(
+    mu_in, entry_in, h_same, h_cross, tabs, own, got, swapped, near, near_swapped,
+    keep, send, mu, entry, tr, ti, sems,
+):
+    count = mu.shape[0]
+    mu_copy, entry_copy = start_all(((mu_in, mu), (entry_in, entry)), sems)
     left = 3 - lax.axis_index("gz")
-
-    def set_t(ref):
+    core = lax.axis_index("angle") % 2
+
+    def set_t(ref, at=slice(None)):
         c, s = half_range_cos_sin(PHASE_GAIN * ref[...])
-        tr[...] = c
-        ti[...] = s
+        tr[at, :] = c
+        ti[at, :] = s
+
+    def set_t_for(step):
+        one_above = (left != 2) & (left - step == 1)
+        here = (step % 2) == core
+        pl.when(~one_above & here)(lambda: set_t(got))
+        pl.when(~one_above & ~here)(lambda: set_t(swapped))
+
+        @pl.when(one_above)
+        def _():
+            set_t(near, pl.ds(pl.multiple_of(core * 128, 128), 128))
+            set_t(near_swapped, pl.ds(pl.multiple_of(128 - core * 128, 128), 128))
 
     def load_from(angle):
         def load(p):
@@ -216,10 +238,11 @@
 
         return load
 
+    set_t_for(0)
+    mu_copy.wait()
+
     def one_slab(step, carry):
-        ahead = left - step
-        for distance, ref in ((3, far), (2, mid), (1, near)):
-            pl.when(ahead == distance)(lambda ref=ref: set_t(ref))
+        pl.when(step > 0)(lambda: set_t_for(step))
         adjoint_step(
             [load_from(n) for n in range(count)],
             [store_into(mu, n) for n in range(count)],
@@ -231,7 +254,7 @@
 
     lax.fori_loop(0, left, one_slab, 0)
     set_t(own)
-    other = 1 - lax.axis_index("angle") % 2
+    entry_copy.wait()
 
     def terms(at):
         gr = gi = 0.0
@@ -243,14 +266,15 @@
         return PHASE_GAIN * (tr[at, :] * gi - ti[at, :] * gr)
 
     for at in range(0, 128, 32):
-        keep[pl.ds(at, 32), :] = terms(pl.ds(pl.multiple_of(128 - 128 * other + at, 32), 32))
-        send[pl.ds(at, 32), :] = terms(pl.ds(pl.multiple_of(128 * other + at, 32), 32))
-
-
-def call(kernel, out_shape, scratch=()):
+        keep[pl.ds(at, 32), :] = terms(pl.ds(pl.multiple_of(core * 128 + at, 32), 32))
+        send[pl.ds(at, 32), :] = terms(pl.ds(pl.multiple_of(128 - core * 128 + at, 32), 32))
+
+
+def call(kernel, in_hbm, out_shape, scratch):
     return pl.pallas_call(
         kernel,
         out_shape=out_shape,
+        in_specs=[pl.BlockSpec(memory_space=pl.ANY if far else pltpu.VMEM) for far in in_hbm],
         scratch_shapes=list(scratch),
         compiler_params=pltpu.CompilerParams(vmem_limit_bytes=VMEM_BYTES),
     )
@@ -268,27 +292,51 @@
     return pairs
 
 
+def slab_pairs(moves):
+    pairs = []
+    for gz, core, gz_to, core_to, flip in moves:
+        for n in range(core, 64, 2):
+            pairs.append((gz * 64 + n, gz_to * 64 + ((n - core + core_to) ^ (32 * flip))))
+    return pairs
+
+
 def per_device(index, prop_phase, entry_field, exit_cotangent):
     count = exit_cotangent.shape[0]
     tabs = jnp.asarray(transform_tables(256))
     own = index[0]
-    near, mid, far = [
-        lax.ppermute(own, "gz", [(n, n - by) for n in range(by, 4)]) for by in (1, 2, 3)
-    ]
+    core = lax.axis_index("angle") % 2
+    swap = angle_pairs(lambda z, y, x, c: (z, y, x, 1 - c))
+    got = lax.ppermute(
+        own,
+        ("gz", "angle"),
+        slab_pairs(((3, 0, 0, 0, 1), (2, 0, 0, 1, 0), (3, 1, 1, 0, 1), (2, 1, 1, 1, 0))),
+    )
+    mine = lax.dynamic_slice_in_dim(own, core * 128, 128, 0)
+    near = lax.ppermute(
+        mine,
+        ("gz", "angle"),
+        slab_pairs(((1, 0, 0, 0, 0), (1, 1, 0, 1, 0), (3, 0, 2, 0, 0), (3, 1, 2, 1, 0))),
+    )
+    field = (count, 2, 256, 256)
+    h_shape = (4, 256, 128)
     mu, h_same, h_cross = call(
         first_kernel,
-        (f32(count, 2, 256, 256), f32(4, 256, 128), f32(4, 256, 128)),
-        (pltpu.VMEM((512, 128), jnp.float32),),
+        (False,) * 3,
+        (f32(*field), f32(*h_shape), f32(*h_shape)),
+        [pltpu.VMEM((512, 128), jnp.float32)],
     )(exit_cotangent, prop_phase, tabs)
+    got, near, mu = lax.optimization_barrier((got, near, mu))
+    swapped = lax.ppermute(got, "angle", swap)
+    near_swapped = lax.ppermute(near, "angle", swap)
+    fields = pltpu.VMEM(field, jnp.float32)
     plane = pltpu.VMEM((256, 256), jnp.float32)
     keep, send = call(
         rest_kernel,
+        (True,) * 2 + (False,) * 8,
         (f32(128, 256), f32(128, 256)),
-        (pltpu.VMEM((count, 2, 256, 256), jnp.float32), plane, plane),
-    )(mu, h_same, h_cross, tabs, entry_field[0], own, near, mid, far)
-
-    core = lax.axis_index("angle") % 2
-    swap = angle_pairs(lambda z, y, x, c: (z, y, x, 1 - c))
+        [fields, fields, plane, plane, pltpu.SemaphoreType.DMA((2,))],
+    )(mu, entry_field[0], h_same, h_cross, tabs, own, got, swapped, near, near_swapped)
+
     total = keep + lax.ppermute(send, "angle", swap)
     for partner in (
         lambda z, y, x, c: (z, y, x ^ 1, c),
@@ -299,7 +347,6 @@
     ):
         total = total + lax.ppermute(total, "angle", angle_pairs(partner))
     angles = count * lax.axis_size("angle")
-    mine = lax.dynamic_slice_in_dim(own, core * 128, 128, 0)
     new = jnp.maximum(mine - UPDATE_RATE * (total / angles), 0.0)
     other = lax.ppermute(new, "angle", swap)
     return jnp.where(

time: 83.1 us -> 64.1 us (0.77)
  waiting for transfers between devices: 34.2 us -> 17.8 us
  Pallas kernels: 22.8 us -> 15.3 us
  local copies, waits for them, and re-layouts: 0.8 us -> 5.06 us
  starting transfers between devices: 23.3 us -> 24.9 us
  other arithmetic: 1.74 us -> 0.84 us
    ppermute x3 -> x4, waiting for transfers between devices: 17.3 us -> 2.47 us  [the longest x1 1.35 us: per_device(): near_swapped = lax.ppermute(near, 'angle', swap)]
    pallas_call x2, Pallas kernels: 22.8 us -> 15.3 us  [the longest x1 11.5 us: per_device(): call(rest_kernel, (True,) * 2 + (False,) * 8, (f32(128, 256), f32(128, 25...]
    unnamed x8 -> x12, local copies, waits for them, and re-layouts: 0.8 us -> 4.14 us
    ppermute x1, starting transfers between devices: 4.12 us -> 5.54 us  [per_device(): other = lax.ppermute(new, 'angle', swap)]
    ppermute x5, waiting for transfers between devices: 14.7 us -> 13.3 us  [per_device(): total = total + lax.ppermute(total, 'angle', angle_pairs(partner))]
    ppermute x3 -> x4, starting transfers between devices: 3.86 us -> 5.11 us  [the longest x1 2.54 us: per_device(): swapped = lax.ppermute(got, 'angle', swap)]
    dynamic_slice x0 -> x1, local copies, waits for them, and re-layouts: none -> 0.92 us  [per_device(): mine = lax.dynamic_slice_in_dim(own, core * 128, 128, 0)]
    add x1, other arithmetic: 0.92 us -> 0.02 us  [per_device(): total = keep + lax.ppermute(send, 'angle', swap)]
  transfers between devices with their start and end apart: 10 -> 11, of which waited for: 8 -> 9; matrix products, arithmetic and copies ran while one was open for 0% -> 1% of each run, Pallas kernels for 9% -> 6%
where the time goes in v2:
time: 64.1 us; the launch traced here: 63.9 us
  starting transfers between devices  24.9 us (39%)
  waiting for transfers between devices  17.8 us (28%)
  Pallas kernels  15.3 us (24%)
  local copies, waits for them, and re-layouts  5.06 us (8%)
  other arithmetic  0.84 us (1%)
    ppermute x5, starting transfers between devices, per_device(): total = total + lax.ppermute(total, 'angle', angle_pairs(partner))  13.8 us
    ppermute x5, waiting for transfers between devices, per_device(): total = total + lax.ppermute(total, 'angle', angle_pairs(partner))  13.3 us
    pallas_call x1, Pallas kernels, per_device(): call(rest_kernel, (True,) * 2 + (False,) * 8, (f32(128, 256), f32(128, 25...  11.5 us
    ppermute x1, starting transfers between devices, per_device(): other = lax.ppermute(new, 'angle', swap)  5.54 us
    unnamed x12, local copies, waits for them, and re-layouts  4.14 us
    pallas_call x1, Pallas kernels, per_device(): call(first_kernel, (False,) * 3, (f32(*field), f32(*h_shape), f32(*h_shap...  3.8 us
    ppermute x1, starting transfers between devices, per_device(): swapped = lax.ppermute(got, 'angle', swap)  2.54 us
    ppermute x1, waiting for transfers between devices, per_device(): near_swapped = lax.ppermute(near, 'angle', swap)  1.35 us
  transfers between devices with their start and end apart: 11, of which 9 were waited for; matrix products, arithmetic and copies ran while one was open for 1% of the time, Pallas kernels for 6%

profile of v2, /device:TPU:1, one launch (start us, length us, event | category | flops | bytes accessed | tf_op | source)
XLA Modules:
  0.0 63.9 jit_solution(6038436333400307044)
XLA Ops:
  0.0 1.3 %collective-permute-start = (f32[256,256]{1,0:T(8,128)}, f32[256,256]{1,0:T(8,128)S(1)}, u32[]{:S(2)}, u32[]{:S(2)}) collective-permute-start(f32[256,256]{1,0:T(8,128)} %bitcast.9), channel_id=1, source_target_pairs={{192,32},{194,34},{196,36},{198,38},{200,40},{202,42},{204,44},{20... | collective-permute-start | bytes 786440 | tf_op jit(solution)/shard_map/ppermute | solution.py:309
  1.3 0.9 %dynamic-slice_bitcast_fusion = f32[128,256]{1,0:T(8,128)S(1)} fusion(f32[1,256,256]{2,1,0:T(8,128)} %param.5, s32[]{:T(128)S(6)} %select_n.27), kind=kLoop, calls=%fused_computation.2 | loop fusion | bytes 262148 | tf_op jit(solution)/shard_map/dynamic_slice | solution.py:314
  2.2 1.3 %collective-permute-start.1 = (f32[128,256]{1,0:T(8,128)S(1)}, f32[128,256]{1,0:T(8,128)S(1)}, u32[]{:S(2)}, u32[]{:S(2)}) collective-permute-start(f32[128,256]{1,0:T(8,128)S(1)} %dynamic-slice_bitcast_fusion), channel_id=1, source_target_pairs={{64,0},{66,2},{68,4},{70,6},{72,8},{74,10},{76,12},{78,14},{80,16}... | collective-permute-start | bytes 393224 | tf_op jit(solution)/shard_map/ppermute | solution.py:315
  3.5 0.0 copy-start
  3.5 1.6 %copy-done = bf16[4,4,256,256]{3,2,1,0:T(8,128)(2,1)S(1)} copy-done((bf16[4,4,256,256]{3,2,1,0:T(8,128)(2,1)S(1)}, bf16[4,4,256,256]{3,2,1,0:T(8,128)(2,1)}, u32[]{:S(2)}) %copy-start) | copy-done | bytes 2097176
  5.1 0.0 copy-start.2
  5.1 1.6 %copy-done.2 = f32[4,2,256,256]{3,2,1,0:T(8,128)S(1)} copy-done((f32[4,2,256,256]{3,2,1,0:T(8,128)S(1)}, f32[4,2,256,256]{3,2,1,0:T(8,128)}, u32[]{:S(2)}) %copy-start.2) | copy-done | bytes 2097176
  6.7 0.0 copy-start.5
  6.7 0.9 %copy-done.5 = f32[256,256]{1,0:T(8,128)S(1)} copy-done((f32[256,256]{1,0:T(8,128)S(1)}, f32[256,256]{1,0:T(8,128)}, u32[]{:S(2)}) %copy-start.5) | copy-done | bytes 262168
  7.7 0.0 copy-start.1
  7.7 0.0 copy-start.3
  7.7 0.0 copy-start.4
  7.7 3.8 %shard_map.55 = (f32[4,2,256,256]{3,2,1,0:T(8,128)S(1)}, f32[4,256,128]{2,1,0:T(8,128)S(1)}, f32[4,256,128]{2,1,0:T(8,128)S(1)}) custom-call(f32[4,2,256,256]{3,2,1,0:T(8,128)S(1)} %copy-done.2, f32[256,256]{1,0:T(8,128)S(1)} %copy-done.5, bf16[4,4,256,256]{3,2,1,0:T(8,128)(2,1)S(1)} %copy-done), custom_call_target="tpu_custom_call" | custom-call | tf_op jit(solution)/shard_map/pallas_call | solution.py:322
  11.5 0.0 collective-permute-done.1.near
  11.5 1.1 %collective-permute-done.got = f32[256,256]{1,0:T(8,128)S(1)} collective-permute-done((f32[256,256]{1,0:T(8,128)}, f32[256,256]{1,0:T(8,128)S(1)}, u32[]{:S(2)}, u32[]{:S(2)}) %collective-permute-start) | collective-permute-done | bytes 262176 | tf_op jit(solution)/shard_map/ppermute | solution.py:309
  12.6 2.5 %collective-permute-start.2 = (f32[256,256]{1,0:T(8,128)S(1)}, f32[256,256]{1,0:T(8,128)S(1)}, u32[]{:S(2)}, u32[]{:S(2)}) collective-permute-start(f32[256,256]{1,0:T(8,128)S(1)} %collective-permute-done.got), channel_id=1, source_target_pairs={{0,1},{1,0},{2,3},{3,2},{4,5},{5,4},{6,7},{7,6},{8,9},{9,8},{10,11... | collective-permute-start | bytes 786440 | tf_op jit(solution)/shard_map/ppermute | solution.py:329
  15.1 0.0 collective-permute-start.3
  15.1 1.3 %collective-permute-done.3.near_swapped = f32[128,256]{1,0:T(8,128)S(1)} collective-permute-done((f32[128,256]{1,0:T(8,128)S(1)}, f32[128,256]{1,0:T(8,128)S(1)}, u32[]{:S(2)}, u32[]{:S(2)}) %collective-permute-start.3) | collective-permute-done | bytes 131104 | tf_op jit(solution)/shard_map/ppermute | solution.py:330
  16.5 0.0 collective-permute-done.2.swapped
  16.5 0.0 copy-done.1
  16.5 0.0 copy-done.3
  16.5 0.0 copy-done.4
  16.5 11.5 %shard_map.56 = (f32[128,256]{1,0:T(8,128)S(1)}, f32[128,256]{1,0:T(8,128)S(1)}) custom-call(f32[4,2,256,256]{3,2,1,0:T(8,128)S(1)} %get-tuple-element.14.mu_in, f32[4,2,256,256]{3,2,1,0:T(8,128)S(1)} %bitcast.8, f32[4,256,128]{2,1,0:T(8,128)S(1)} %get-tuple-element.15.h_same, f32[4,256,128]{2,1,0:T(8,128)S(1)} %get-tuple-element.16.h_cross, ...), custom_call_target="tpu_custom_call" | custom-call | tf_op jit(solution)/shard_map/pallas_call | solution.py:333
  28.0 0.5 collective-permute-start.4
  28.4 1.0 %collective-permute-done.4 = f32[128,256]{1,0:T(8,128)S(1)} collective-permute-done((f32[128,256]{1,0:T(8,128)S(1)}, f32[128,256]{1,0:T(8,128)S(1)}, u32[]{:S(2)}, u32[]{:S(2)}) %collective-permute-start.4) | collective-permute-done | bytes 131104 | tf_op jit(solution)/shard_map/ppermute | solution.py:340
  29.5 1.3 %collective-permute-start.5 = (f32[128,256]{1,0:T(8,128)S(1)}, f32[128,256]{1,0:T(8,128)S(1)}, u32[]{:S(2)}, u32[]{:S(2)}) collective-permute-start(f32[128,256]{1,0:T(8,128)S(1)} %add.27), channel_id=1, source_target_pairs={{0,2},{1,3},{2,0},{3,1},{4,6},{5,7},{6,4},{7,5},{8,10},{9,11},{10,... | collective-permute-start | bytes 393224 | tf_op jit(solution)/shard_map/ppermute | solution.py:348
  30.7 3.5 %collective-permute-done.5 = f32[128,256]{1,0:T(8,128)S(1)} collective-permute-done((f32[128,256]{1,0:T(8,128)S(1)}, f32[128,256]{1,0:T(8,128)S(1)}, u32[]{:S(2)}, u32[]{:S(2)}) %collective-permute-start.5) | collective-permute-done | bytes 131104 | tf_op jit(solution)/shard_map/ppermute | solution.py:348
  34.3 2.6 %collective-permute-start.6 = (f32[128,256]{1,0:T(8,128)S(1)}, f32[128,256]{1,0:T(8,128)S(1)}, u32[]{:S(2)}, u32[]{:S(2)}) collective-permute-start(f32[128,256]{1,0:T(8,128)S(1)} %add.28), channel_id=1, source_target_pairs={{0,6},{1,7},{2,4},{3,5},{4,2},{5,3},{6,0},{7,1},{8,14},{9,15},{10,... | collective-permute-start | bytes 393224 | tf_op jit(solution)/shard_map/ppermute | solution.py:348
  36.8 2.6 %collective-permute-done.6 = f32[128,256]{1,0:T(8,128)S(1)} collective-permute-done((f32[128,256]{1,0:T(8,128)S(1)}, f32[128,256]{1,0:T(8,128)S(1)}, u32[]{:S(2)}, u32[]{:S(2)}) %collective-permute-start.6) | collective-permute-done | bytes 131104 | tf_op jit(solution)/shard_map/ppermute | solution.py:348
  39.4 1.4 %collective-permute-start.7 = (f32[128,256]{1,0:T(8,128)S(1)}, f32[128,256]{1,0:T(8,128)S(1)}, u32[]{:S(2)}, u32[]{:S(2)}) collective-permute-start(f32[128,256]{1,0:T(8,128)S(1)} %add.29), channel_id=1, source_target_pairs={{0,8},{1,9},{2,10},{3,11},{4,12},{5,13},{6,14},{7,15},{8,0},{9,1},... | collective-permute-start | bytes 393224 | tf_op jit(solution)/shard_map/ppermute | solution.py:348
  40.8 2.5 %collective-permute-done.7 = f32[128,256]{1,0:T(8,128)S(1)} collective-permute-done((f32[128,256]{1,0:T(8,128)S(1)}, f32[128,256]{1,0:T(8,128)S(1)}, u32[]{:S(2)}, u32[]{:S(2)}) %collective-permute-start.7) | collective-permute-done | bytes 131104 | tf_op jit(solution)/shard_map/ppermute | solution.py:348
  43.3 2.8 %collective-permute-start.8 = (f32[128,256]{1,0:T(8,128)S(1)}, f32[128,256]{1,0:T(8,128)S(1)}, u32[]{:S(2)}, u32[]{:S(2)}) collective-permute-start(f32[128,256]{1,0:T(8,128)S(1)} %add.30), channel_id=1, source_target_pairs={{0,24},{1,25},{2,26},{3,27},{4,28},{5,29},{6,30},{7,31},{8,16},{9,... | collective-permute-start | bytes 393224 | tf_op jit(solution)/shard_map/ppermute | solution.py:348
  46.2 2.4 %collective-permute-done.8 = f32[128,256]{1,0:T(8,128)S(1)} collective-permute-done((f32[128,256]{1,0:T(8,128)S(1)}, f32[128,256]{1,0:T(8,128)S(1)}, u32[]{:S(2)}, u32[]{:S(2)}) %collective-permute-start.8) | collective-permute-done | bytes 131104 | tf_op jit(solution)/shard_map/ppermute | solution.py:348
  48.5 5.7 %collective-permute-start.9 = (f32[128,256]{1,0:T(8,128)S(1)}, f32[128,256]{1,0:T(8,128)S(1)}, u32[]{:S(2)}, u32[]{:S(2)}) collective-permute-start(f32[128,256]{1,0:T(8,128)S(1)} %add.31), channel_id=1, source_target_pairs={{0,32},{1,33},{2,34},{3,35},{4,36},{5,37},{6,38},{7,39},{8,40},{9,... | collective-permute-start | bytes 393224 | tf_op jit(solution)/shard_map/ppermute | solution.py:348
  54.3 2.4 %collective-permute-done.9 = f32[128,256]{1,0:T(8,128)S(1)} collective-permute-done((f32[128,256]{1,0:T(8,128)S(1)}, f32[128,256]{1,0:T(8,128)S(1)}, u32[]{:S(2)}, u32[]{:S(2)}) %collective-permute-start.9) | collective-permute-done | bytes 131104 | tf_op jit(solution)/shard_map/ppermute | solution.py:348
  56.7 5.5 %collective-permute-start.10 = (f32[128,256]{1,0:T(8,128)S(1)}, f32[128,256]{1,0:T(8,128)S(1)}, u32[]{:S(2)}, u32[]{:S(2)}) collective-permute-start(f32[128,256]{1,0:T(8,128)S(1)} %subtract_maximum_fusion), channel_id=1, source_target_pairs={{0,1},{1,0},{2,3},{3,2},{4,5},{5,4},{6,7},{7,6},{8,9},{9,8},{10,11... | collective-permute-start | bytes 393224 | tf_op jit(solution)/shard_map/ppermute | solution.py:351
  62.2 1.0 %collective-permute-done.10 = f32[128,256]{1,0:T(8,128)S(1)} collective-permute-done((f32[128,256]{1,0:T(8,128)S(1)}, f32[128,256]{1,0:T(8,128)S(1)}, u32[]{:S(2)}, u32[]{:S(2)}) %collective-permute-start.10) | collective-permute-done | bytes 131104 | tf_op jit(solution)/shard_map/ppermute | solution.py:351
  63.2 0.7 %maximum_select_fusion = f32[1,256,256]{2,1,0:T(8,128)} fusion(f32[1,128,256]{2,1,0:T(8,128)S(1)} %bitcast.12, f32[1,128,256]{2,1,0:T(8,128)S(1)} %bitcast.11, pred[]{:T(512)S(6)} %eq.5), kind=kLoop, calls=%fused_computation | loop fusion | flops 196608 | bytes 524289 | tf_op jit(solution)/shard_map/jit(_where)/select_n | solution.py:352
  (6 shorter events, 0.1 us)
Async XLA Ops:
  0.0 12.6 %collective-permute-start = (f32[256,256]{1,0:T(8,128)}, f32[256,256]{1,0:T(8,128)S(1)}, u32[]{:S(2)}, u32[]{:S(2)}) collective-permute-start(f32[256,256]{1,0:T(8,128)} %bitcast.9), channel_id=1, source_target_pairs={{192,32},{194,34},{196,36},{198,38},{200,40},{202,42},{204,44},{20... | collective-permute-start | bytes 786440 | tf_op jit(solution)/shard_map/ppermute | solution.py:309
  2.2 9.3 %collective-permute-start.1 = (f32[128,256]{1,0:T(8,128)S(1)}, f32[128,256]{1,0:T(8,128)S(1)}, u32[]{:S(2)}, u32[]{:S(2)}) collective-permute-start(f32[128,256]{1,0:T(8,128)S(1)} %dynamic-slice_bitcast_fusion), channel_id=1, source_target_pairs={{64,0},{66,2},{68,4},{70,6},{72,8},{74,10},{76,12},{78,14},{80,16}... | collective-permute-start | bytes 393224 | tf_op jit(solution)/shard_map/ppermute | solution.py:315
  3.5 1.6 %copy-start = (bf16[4,4,256,256]{3,2,1,0:T(8,128)(2,1)S(1)}, bf16[4,4,256,256]{3,2,1,0:T(8,128)(2,1)}, u32[]{:S(2)}) copy-start(bf16[4,4,256,256]{3,2,1,0:T(8,128)(2,1)} %constant.32.clone.tabs) | copy-start | bytes 6291460
  5.1 1.6 %copy-start.2 = (f32[4,2,256,256]{3,2,1,0:T(8,128)S(1)}, f32[4,2,256,256]{3,2,1,0:T(8,128)}, u32[]{:S(2)}) copy-start(f32[4,2,256,256]{3,2,1,0:T(8,128)} %dual.1) | copy-start | bytes 6291460
  6.7 0.9 %copy-start.5 = (f32[256,256]{1,0:T(8,128)S(1)}, f32[256,256]{1,0:T(8,128)}, u32[]{:S(2)}) copy-start(f32[256,256]{1,0:T(8,128)} %phase.1) | copy-start | bytes 786436
  7.7 8.8 %copy-start.1 = (bf16[4,4,256,256]{3,2,1,0:T(8,128)(2,1)S(1)}, bf16[4,4,256,256]{3,2,1,0:T(8,128)(2,1)}, u32[]{:S(2)}) copy-start(bf16[4,4,256,256]{3,2,1,0:T(8,128)(2,1)} %constant.32.clone.tabs) | copy-start | bytes 6291460
  7.7 8.8 %copy-start.3 = (f32[1,4,2,256,256]{4,3,2,1,0:T(8,128)S(1)}, f32[1,4,2,256,256]{4,3,2,1,0:T(8,128)}, u32[]{:S(2)}) copy-start(f32[1,4,2,256,256]{4,3,2,1,0:T(8,128)} %param.7) | copy-start | bytes 6291460
  7.7 8.8 %copy-start.4 = (f32[1,256,256]{2,1,0:T(8,128)S(1)}, f32[1,256,256]{2,1,0:T(8,128)}, u32[]{:S(2)}) copy-start(f32[1,256,256]{2,1,0:T(8,128)} %param.5) | copy-start | bytes 786436
  12.6 3.9 %collective-permute-start.2 = (f32[256,256]{1,0:T(8,128)S(1)}, f32[256,256]{1,0:T(8,128)S(1)}, u32[]{:S(2)}, u32[]{:S(2)}) collective-permute-start(f32[256,256]{1,0:T(8,128)S(1)} %collective-permute-done.got), channel_id=1, source_target_pairs={{0,1},{1,0},{2,3},{3,2},{4,5},{5,4},{6,7},{7,6},{8,9},{9,8},{10,11... | collective-permute-start | bytes 786440 | tf_op jit(solution)/shard_map/ppermute | solution.py:329
  15.1 1.3 %collective-permute-start.3 = (f32[128,256]{1,0:T(8,128)S(1)}, f32[128,256]{1,0:T(8,128)S(1)}, u32[]{:S(2)}, u32[]{:S(2)}) collective-permute-start(f32[128,256]{1,0:T(8,128)S(1)} %collective-permute-done.1.near), channel_id=1, source_target_pairs={{0,1},{1,0},{2,3},{3,2},{4,5},{5,4},{6,7},{7,6},{8,9},{9,8},{10,11... | collective-permute-start | bytes 393224 | tf_op jit(solution)/shard_map/ppermute | solution.py:330
  28.0 1.5 %collective-permute-start.4 = (f32[128,256]{1,0:T(8,128)S(1)}, f32[128,256]{1,0:T(8,128)S(1)}, u32[]{:S(2)}, u32[]{:S(2)}) collective-permute-start(f32[128,256]{1,0:T(8,128)S(1)} %get-tuple-element.20), channel_id=1, source_target_pairs={{0,1},{1,0},{2,3},{3,2},{4,5},{5,4},{6,7},{7,6},{8,9},{9,8},{10,11... | collective-permute-start | bytes 393224 | tf_op jit(solution)/shard_map/ppermute | solution.py:340
  29.5 4.8 %collective-permute-start.5 = (f32[128,256]{1,0:T(8,128)S(1)}, f32[128,256]{1,0:T(8,128)S(1)}, u32[]{:S(2)}, u32[]{:S(2)}) collective-permute-start(f32[128,256]{1,0:T(8,128)S(1)} %add.27), channel_id=1, source_target_pairs={{0,2},{1,3},{2,0},{3,1},{4,6},{5,7},{6,4},{7,5},{8,10},{9,11},{10,... | collective-permute-start | bytes 393224 | tf_op jit(solution)/shard_map/ppermute | solution.py:348
  34.3 5.1 %collective-permute-start.6 = (f32[128,256]{1,0:T(8,128)S(1)}, f32[128,256]{1,0:T(8,128)S(1)}, u32[]{:S(2)}, u32[]{:S(2)}) collective-permute-start(f32[128,256]{1,0:T(8,128)S(1)} %add.28), channel_id=1, source_target_pairs={{0,6},{1,7},{2,4},{3,5},{4,2},{5,3},{6,0},{7,1},{8,14},{9,15},{10,... | collective-permute-start | bytes 393224 | tf_op jit(solution)/shard_map/ppermute | solution.py:348
  39.4 3.9 %collective-permute-start.7 = (f32[128,256]{1,0:T(8,128)S(1)}, f32[128,256]{1,0:T(8,128)S(1)}, u32[]{:S(2)}, u32[]{:S(2)}) collective-permute-start(f32[128,256]{1,0:T(8,128)S(1)} %add.29), channel_id=1, source_target_pairs={{0,8},{1,9},{2,10},{3,11},{4,12},{5,13},{6,14},{7,15},{8,0},{9,1},... | collective-permute-start | bytes 393224 | tf_op jit(solution)/shard_map/ppermute | solution.py:348
  43.3 5.2 %collective-permute-start.8 = (f32[128,256]{1,0:T(8,128)S(1)}, f32[128,256]{1,0:T(8,128)S(1)}, u32[]{:S(2)}, u32[]{:S(2)}) collective-permute-start(f32[128,256]{1,0:T(8,128)S(1)} %add.30), channel_id=1, source_target_pairs={{0,24},{1,25},{2,26},{3,27},{4,28},{5,29},{6,30},{7,31},{8,16},{9,... | collective-permute-start | bytes 393224 | tf_op jit(solution)/shard_map/ppermute | solution.py:348
  48.5 8.1 %collective-permute-start.9 = (f32[128,256]{1,0:T(8,128)S(1)}, f32[128,256]{1,0:T(8,128)S(1)}, u32[]{:S(2)}, u32[]{:S(2)}) collective-permute-start(f32[128,256]{1,0:T(8,128)S(1)} %add.31), channel_id=1, source_target_pairs={{0,32},{1,33},{2,34},{3,35},{4,36},{5,37},{6,38},{7,39},{8,40},{9,... | collective-permute-start | bytes 393224 | tf_op jit(solution)/shard_map/ppermute | solution.py:348
  56.7 6.5 %collective-permute-start.10 = (f32[128,256]{1,0:T(8,128)S(1)}, f32[128,256]{1,0:T(8,128)S(1)}, u32[]{:S(2)}, u32[]{:S(2)}) collective-permute-start(f32[128,256]{1,0:T(8,128)S(1)} %subtract_maximum_fusion), channel_id=1, source_target_pairs={{0,1},{1,0},{2,3},{3,2},{4,5},{5,4},{6,7},{7,6},{8,9},{9,8},{10,11... | collective-permute-start | bytes 393224 | tf_op jit(solution)/shard_map/ppermute | solution.py:351

commit v3 on v2

--- a/solution.py
+++ b/solution.py
@@ -1,7 +1,7 @@
+import math
+
 import jax
 import jax.numpy as jnp
-import ml_dtypes
-import numpy as np
 from jax import lax
 from jax.experimental import pallas as pl
 from jax.experimental.pallas import tpu as pltpu
@@ -12,40 +12,29 @@
 VMEM_BYTES = 28 * 2**20
 
 
-def two_terms(matrix):
-    matrix = matrix.astype(np.float32)
-    high = matrix.astype(ml_dtypes.bfloat16)
-    low = (matrix - high.astype(np.float32)).astype(ml_dtypes.bfloat16)
-    return high, low, np.zeros_like(low)
-
-
-def transform_tables(grid_len):
-    quarter = grid_len // 4
-    j = np.arange(quarter)
-    left_fwd, right_fwd, right_inv, left_inv = [], [], [], []
-
-    def as_real(matrix):
-        return np.block([[matrix.real, -matrix.imag], [matrix.imag, matrix.real]])
-
-    def on_left(matrix):
-        high, low, zero = two_terms(matrix)
-        return np.block([[high, high], [low, zero]])
-
-    def on_right(matrix):
-        high, low, zero = two_terms(matrix)
-        return np.block([[high, low], [high, zero]])
-
-    for residue in range(4):
-        turns = (residue * j[None, :]) / grid_len + (j[:, None] * j[None, :] % quarter) / quarter
-        fwd = np.exp(-2j * np.pi * turns) / np.sqrt(grid_len)
-        inv = np.conj(fwd).T
-        flip = np.where(j.repeat(2) < 0, 0.0, 1.0)
-        flip[quarter:] = -1.0 if residue in (1, 2) else 1.0
-        left_fwd.append(on_left(as_real(fwd)))
-        right_fwd.append(on_right(as_real(fwd).T * flip[:, None]))
-        right_inv.append(on_right(as_real(inv).T * flip[None, :]))
-        left_inv.append(on_left(as_real(inv)))
-    return np.stack([np.stack(m) for m in (left_fwd, right_fwd, right_inv, left_inv)])
+def tables_kernel(tabs):
+    row = lax.broadcasted_iota(jnp.int32, (128, 128), 0)
+    lane = lax.broadcasted_iota(jnp.int32, (128, 128), 1)
+    zero = jnp.zeros((128, 128), jnp.bfloat16)
+    for n in range(4):
+        for which in range(2):
+            m, j = (row % 64, lane % 64) if which == 0 else (lane % 64, row % 64)
+            turn = (n * j + 4 * m * j + 128) % 256 - 128
+            c, s = half_range_cos_sin(turn.astype(jnp.float32) * (math.pi / 256.0))
+            cos, sin = (1.0 - 2.0 * s * s) / 16.0, 2.0 * s * c / 16.0
+            upper, right = row < 64, lane >= 64
+            cross = jnp.where(upper, sin, -sin)
+            real = jnp.where(upper != right, cos, cross if which == 0 else -cross)
+            for to in ((0, 2), (3, 1))[which]:
+                flipped = real
+                if n in (1, 2) and to in (1, 2):
+                    flipped = jnp.where((row if to == 1 else lane) < 64, real, -real)
+                high, low = split(flipped)
+                on_left = to in (0, 3)
+                tabs[to, n, :128, :128] = high
+                tabs[to, n, :128, 128:] = high if on_left else low
+                tabs[to, n, 128:, :128] = low if on_left else high
+                tabs[to, n, 128:, 128:] = zero
 
 
 def split(block):
@@ -302,7 +291,6 @@
 
 def per_device(index, prop_phase, entry_field, exit_cotangent):
     count = exit_cotangent.shape[0]
-    tabs = jnp.asarray(transform_tables(256))
     own = index[0]
     core = lax.axis_index("angle") % 2
     swap = angle_pairs(lambda z, y, x, c: (z, y, x, 1 - c))
@@ -319,6 +307,9 @@
     )
     field = (count, 2, 256, 256)
     h_shape = (4, 256, 128)
+    tabs = call(
+        tables_kernel, (), jax.ShapeDtypeStruct((4, 4, 256, 256), jnp.bfloat16), ()
+    )()
     mu, h_same, h_cross = call(
         first_kernel,
         (False,) * 3,
@@ -338,14 +329,20 @@
     )(mu, entry_field[0], h_same, h_cross, tabs, own, got, swapped, near, near_swapped)
 
     total = keep + lax.ppermute(send, "angle", swap)
-    for partner in (
-        lambda z, y, x, c: (z, y, x ^ 1, c),
-        lambda z, y, x, c: (z, y, 3 - x, c),
-        lambda z, y, x, c: (z, y ^ 1, x, c),
-        lambda z, y, x, c: (z, 3 - y, x, c),
-        lambda z, y, x, c: (1 - z, y, x, c),
+    for ring in (
+        (
+            lambda z, y, x, c: (z, y, x ^ 2, c),
+            lambda z, y, x, c: (z, y, 3 - x, c),
+            lambda z, y, x, c: (z, y, x ^ 1, c),
+        ),
+        (
+            lambda z, y, x, c: (z, y ^ 2, x, c),
+            lambda z, y, x, c: (z, 3 - y, x, c),
+            lambda z, y, x, c: (z, y ^ 1, x, c),
+        ),
+        (lambda z, y, x, c: (1 - z, y, x, c),),
     ):
-        total = total + lax.ppermute(total, "angle", angle_pairs(partner))
+        total = total + sum(lax.ppermute(total, "angle", angle_pairs(p)) for p in ring)
     angles = count * lax.axis_size("angle")
     new = jnp.maximum(mine - UPDATE_RATE * (total / angles), 0.0)
     other = lax.ppermute(new, "angle", swap)

time: 64.1 us -> 62.6 us (0.977)
  local copies, waits for them, and re-layouts: 5.06 us -> 0.94 us
  waiting for transfers between devices: 17.8 us -> 21.7 us
  starting transfers between devices: 24.9 us -> 22.6 us
  Pallas kernels: 15.3 us -> 16.3 us
    unnamed x12 -> x8, local copies, waits for them, and re-layouts: 4.14 us -> 0.02 us
    ppermute x1, starting transfers between devices: 5.54 us -> 3.25 us  [per_device(): other = lax.ppermute(new, 'angle', swap)]
    ppermute x1, waiting for transfers between devices: 1.12 us -> 2.98 us  [per_device(): lax.ppermute(own, ('gz', 'angle'), slab_pairs(((3, 0, 0, 0, 1), (2, 0, 0,...]
    ppermute x1, waiting for transfers between devices: 0.01 us -> 1.19 us  [per_device(): lax.ppermute(mine, ('gz', 'angle'), slab_pairs(((1, 0, 0, 0, 0), (1, 1, 0...]
    pallas_call x0 -> x1, Pallas kernels: none -> 1.06 us  [per_device(): call(tables_kernel, (), jax.ShapeDtypeStruct((4, 4, 256, 256), jnp.bfloat...]
    ppermute x5 -> x7, waiting for transfers between devices: 13.3 us -> 14.2 us  [per_device(): lax.ppermute(total, 'angle', angle_pairs(p))]
    ppermute x5 -> x7, starting transfers between devices: 13.8 us -> 13.5 us  [per_device(): lax.ppermute(total, 'angle', angle_pairs(p))]
  transfers between devices with their start and end apart: 11 -> 13, of which waited for: 9 -> 11; matrix products, arithmetic and copies ran while one was open for 1% -> 1% of each run, Pallas kernels for 6% -> 8%
where the time goes in v3:
time: 62.6 us; the launch traced here: 62.5 us
  starting transfers between devices  22.6 us (36%)
  waiting for transfers between devices  21.7 us (35%)
  Pallas kernels  16.3 us (26%)
  local copies, waits for them, and re-layouts  0.94 us (2%)
  other arithmetic  0.84 us (1%)
    ppermute x7, waiting for transfers between devices, per_device(): lax.ppermute(total, 'angle', angle_pairs(p))  14.2 us
    ppermute x7, starting transfers between devices, per_device(): lax.ppermute(total, 'angle', angle_pairs(p))  13.5 us
    pallas_call x1, Pallas kernels, per_device(): call(rest_kernel, (True,) * 2 + (False,) * 8, (f32(128, 256), f32(128, 25...  11.5 us
    pallas_call x1, Pallas kernels, per_device(): call(first_kernel, (False,) * 3, (f32(*field), f32(*h_shape), f32(*h_shap...  3.79 us
    ppermute x1, starting transfers between devices, per_device(): other = lax.ppermute(new, 'angle', swap)  3.25 us
    ppermute x1, waiting for transfers between devices, per_device(): lax.ppermute(own, ('gz', 'angle'), slab_pairs(((3, 0, 0, 0, 1), (2, 0, 0,...  2.98 us
    ppermute x1, starting transfers between devices, per_device(): swapped = lax.ppermute(got, 'angle', swap)  2.54 us
    ppermute x1, starting transfers between devices, per_device(): lax.ppermute(own, ('gz', 'angle'), slab_pairs(((3, 0, 0, 0, 1), (2, 0, 0,...  1.41 us
  transfers between devices with their start and end apart: 13, of which 11 were waited for; matrix products, arithmetic and copies ran while one was open for 1% of the time, Pallas kernels for 8%

profile of v3, /device:TPU:1, one launch (start us, length us, event | category | flops | bytes accessed | tf_op | source)
XLA Modules:
  0.0 62.5 jit_solution(17974242896185905339)
XLA Ops:
  0.0 0.0 copy-start
  0.0 0.0 copy-start.3
  0.0 1.4 %collective-permute-start = (f32[256,256]{1,0:T(8,128)}, f32[256,256]{1,0:T(8,128)S(1)}, u32[]{:S(2)}, u32[]{:S(2)}) collective-permute-start(f32[256,256]{1,0:T(8,128)} %bitcast.9), channel_id=1, source_target_pairs={{192,32},{194,34},{196,36},{198,38},{200,40},{202,42},{204,44},{20... | collective-permute-start | bytes 786440 | tf_op jit(solution)/shard_map/ppermute | solution.py:297
  1.4 0.9 %dynamic-slice_bitcast_fusion = f32[128,256]{1,0:T(8,128)S(1)} fusion(f32[1,256,256]{2,1,0:T(8,128)} %param.4, s32[]{:T(128)S(6)} %select_n.27), kind=kLoop, calls=%fused_computation.4 | loop fusion | bytes 262148 | tf_op jit(solution)/shard_map/dynamic_slice | solution.py:302
  2.4 1.3 %collective-permute-start.1 = (f32[128,256]{1,0:T(8,128)S(1)}, f32[128,256]{1,0:T(8,128)S(1)}, u32[]{:S(2)}, u32[]{:S(2)}) collective-permute-start(f32[128,256]{1,0:T(8,128)S(1)} %dynamic-slice_bitcast_fusion), channel_id=1, source_target_pairs={{64,0},{66,2},{68,4},{70,6},{72,8},{74,10},{76,12},{78,14},{80,16}... | collective-permute-start | bytes 393224 | tf_op jit(solution)/shard_map/ppermute | solution.py:303
  3.7 1.1 %shard_map.46.tabs = bf16[4,4,256,256]{3,2,1,0:T(8,128)(2,1)S(1)} custom-call(), custom_call_target="tpu_custom_call" | custom-call | tf_op jit(solution)/shard_map/pallas_call | solution.py:310
  4.7 0.0 copy-done
  4.7 0.0 copy-done.3
  4.7 0.0 copy-start.1
  4.8 0.0 copy-start.2
  4.8 3.8 %shard_map.47 = (f32[4,2,256,256]{3,2,1,0:T(8,128)S(1)}, f32[4,256,128]{2,1,0:T(8,128)S(1)}, f32[4,256,128]{2,1,0:T(8,128)S(1)}) custom-call(f32[4,2,256,256]{3,2,1,0:T(8,128)S(1)} %copy-done, f32[256,256]{1,0:T(8,128)S(1)} %copy-done.3, bf16[4,4,256,256]{3,2,1,0:T(8,128)(2,1)S(1)} %shard_map.46.tabs), custom_call_target="tpu_custom_call" | custom-call | tf_op jit(solution)/shard_map/pallas_call | solution.py:313
  8.6 1.2 %collective-permute-done.1.near = f32[128,256]{1,0:T(8,128)S(1)} collective-permute-done((f32[128,256]{1,0:T(8,128)S(1)}, f32[128,256]{1,0:T(8,128)S(1)}, u32[]{:S(2)}, u32[]{:S(2)}) %collective-permute-start.1) | collective-permute-done | bytes 131104 | tf_op jit(solution)/shard_map/ppermute | solution.py:303
  9.8 3.0 %collective-permute-done.got = f32[256,256]{1,0:T(8,128)S(1)} collective-permute-done((f32[256,256]{1,0:T(8,128)}, f32[256,256]{1,0:T(8,128)S(1)}, u32[]{:S(2)}, u32[]{:S(2)}) %collective-permute-start) | collective-permute-done | bytes 262176 | tf_op jit(solution)/shard_map/ppermute | solution.py:297
  12.7 2.5 %collective-permute-start.2 = (f32[256,256]{1,0:T(8,128)S(1)}, f32[256,256]{1,0:T(8,128)S(1)}, u32[]{:S(2)}, u32[]{:S(2)}) collective-permute-start(f32[256,256]{1,0:T(8,128)S(1)} %collective-permute-done.got), channel_id=1, source_target_pairs={{0,1},{1,0},{2,3},{3,2},{4,5},{5,4},{6,7},{7,6},{8,9},{9,8},{10,11... | collective-permute-start | bytes 786440 | tf_op jit(solution)/shard_map/ppermute | solution.py:320
  15.3 0.0 collective-permute-start.3
  15.3 1.3 %collective-permute-done.3.near_swapped = f32[128,256]{1,0:T(8,128)S(1)} collective-permute-done((f32[128,256]{1,0:T(8,128)S(1)}, f32[128,256]{1,0:T(8,128)S(1)}, u32[]{:S(2)}, u32[]{:S(2)}) %collective-permute-start.3) | collective-permute-done | bytes 131104 | tf_op jit(solution)/shard_map/ppermute | solution.py:321
  16.6 0.0 collective-permute-done.2.swapped
  16.6 0.0 copy-done.1
  16.6 0.0 copy-done.2
  16.6 11.5 %shard_map.48 = (f32[128,256]{1,0:T(8,128)S(1)}, f32[128,256]{1,0:T(8,128)S(1)}) custom-call(f32[4,2,256,256]{3,2,1,0:T(8,128)S(1)} %get-tuple-element.14.mu_in, f32[4,2,256,256]{3,2,1,0:T(8,128)S(1)} %bitcast.8, f32[4,256,128]{2,1,0:T(8,128)S(1)} %get-tuple-element.15.h_same, f32[4,256,128]{2,1,0:T(8,128)S(1)} %get-tuple-element.16.h_cross, ...), custom_call_target="tpu_custom_call" | custom-call | tf_op jit(solution)/shard_map/pallas_call | solution.py:324
  28.1 0.6 %collective-permute-start.4 = (f32[128,256]{1,0:T(8,128)S(1)}, f32[128,256]{1,0:T(8,128)S(1)}, u32[]{:S(2)}, u32[]{:S(2)}) collective-permute-start(f32[128,256]{1,0:T(8,128)S(1)} %get-tuple-element.20), channel_id=1, source_target_pairs={{0,1},{1,0},{2,3},{3,2},{4,5},{5,4},{6,7},{7,6},{8,9},{9,8},{10,11... | collective-permute-start | bytes 393224 | tf_op jit(solution)/shard_map/ppermute | solution.py:331
  28.8 1.0 %collective-permute-done.4 = f32[128,256]{1,0:T(8,128)S(1)} collective-permute-done((f32[128,256]{1,0:T(8,128)S(1)}, f32[128,256]{1,0:T(8,128)S(1)}, u32[]{:S(2)}, u32[]{:S(2)}) %collective-permute-start.4) | collective-permute-done | bytes 131104 | tf_op jit(solution)/shard_map/ppermute | solution.py:331
  29.8 1.3 %collective-permute-start.7 = (f32[128,256]{1,0:T(8,128)S(1)}, f32[128,256]{1,0:T(8,128)S(1)}, u32[]{:S(2)}, u32[]{:S(2)}) collective-permute-start(f32[128,256]{1,0:T(8,128)S(1)} %add.33), channel_id=1, source_target_pairs={{0,2},{1,3},{2,0},{3,1},{4,6},{5,7},{6,4},{7,5},{8,10},{9,11},{10,... | collective-permute-start | bytes 393224 | tf_op jit(solution)/shard_map/ppermute | solution.py:345
  31.1 1.8 %collective-permute-start.6 = (f32[128,256]{1,0:T(8,128)S(1)}, f32[128,256]{1,0:T(8,128)S(1)}, u32[]{:S(2)}, u32[]{:S(2)}) collective-permute-start(f32[128,256]{1,0:T(8,128)S(1)} %add.33), channel_id=1, source_target_pairs={{0,6},{1,7},{2,4},{3,5},{4,2},{5,3},{6,0},{7,1},{8,14},{9,15},{10,... | collective-permute-start | bytes 393224 | tf_op jit(solution)/shard_map/ppermute | solution.py:345
  32.9 0.6 %collective-permute-start.5 = (f32[128,256]{1,0:T(8,128)S(1)}, f32[128,256]{1,0:T(8,128)S(1)}, u32[]{:S(2)}, u32[]{:S(2)}) collective-permute-start(f32[128,256]{1,0:T(8,128)S(1)} %add.33), channel_id=1, source_target_pairs={{0,4},{1,5},{2,6},{3,7},{4,0},{5,1},{6,2},{7,3},{8,12},{9,13},{10,... | collective-permute-start | bytes 393224 | tf_op jit(solution)/shard_map/ppermute | solution.py:345
  33.5 1.1 %collective-permute-done.7 = f32[128,256]{1,0:T(8,128)S(1)} collective-permute-done((f32[128,256]{1,0:T(8,128)S(1)}, f32[128,256]{1,0:T(8,128)S(1)}, u32[]{:S(2)}, u32[]{:S(2)}) %collective-permute-start.7) | collective-permute-done | bytes 131104 | tf_op jit(solution)/shard_map/ppermute | solution.py:345
  34.6 3.2 %collective-permute-done.6 = f32[128,256]{1,0:T(8,128)S(1)} collective-permute-done((f32[128,256]{1,0:T(8,128)S(1)}, f32[128,256]{1,0:T(8,128)S(1)}, u32[]{:S(2)}, u32[]{:S(2)}) %collective-permute-start.6) | collective-permute-done | bytes 131104 | tf_op jit(solution)/shard_map/ppermute | solution.py:345
  37.7 1.7 %collective-permute-done.5 = f32[128,256]{1,0:T(8,128)S(1)} collective-permute-done((f32[128,256]{1,0:T(8,128)S(1)}, f32[128,256]{1,0:T(8,128)S(1)}, u32[]{:S(2)}, u32[]{:S(2)}) %collective-permute-start.5) | collective-permute-done | bytes 131104 | tf_op jit(solution)/shard_map/ppermute | solution.py:345
  39.5 1.4 %collective-permute-start.10 = (f32[128,256]{1,0:T(8,128)S(1)}, f32[128,256]{1,0:T(8,128)S(1)}, u32[]{:S(2)}, u32[]{:S(2)}) collective-permute-start(f32[128,256]{1,0:T(8,128)S(1)} %add_add_fusion.1), channel_id=1, source_target_pairs={{0,8},{1,9},{2,10},{3,11},{4,12},{5,13},{6,14},{7,15},{8,0},{9,1},... | collective-permute-start | bytes 393224 | tf_op jit(solution)/shard_map/ppermute | solution.py:345
  40.9 1.9 %collective-permute-start.9 = (f32[128,256]{1,0:T(8,128)S(1)}, f32[128,256]{1,0:T(8,128)S(1)}, u32[]{:S(2)}, u32[]{:S(2)}) collective-permute-start(f32[128,256]{1,0:T(8,128)S(1)} %add_add_fusion.1), channel_id=1, source_target_pairs={{0,24},{1,25},{2,26},{3,27},{4,28},{5,29},{6,30},{7,31},{8,16},{9,... | collective-permute-start | bytes 393224 | tf_op jit(solution)/shard_map/ppermute | solution.py:345
  42.8 0.7 %collective-permute-start.8 = (f32[128,256]{1,0:T(8,128)S(1)}, f32[128,256]{1,0:T(8,128)S(1)}, u32[]{:S(2)}, u32[]{:S(2)}) collective-permute-start(f32[128,256]{1,0:T(8,128)S(1)} %add_add_fusion.1), channel_id=1, source_target_pairs={{0,16},{1,17},{2,18},{3,19},{4,20},{5,21},{6,22},{7,23},{8,24},{9,... | collective-permute-start | bytes 393224 | tf_op jit(solution)/shard_map/ppermute | solution.py:345
  43.5 0.0 collective-permute-done.10
  43.5 2.4 %collective-permute-done.9 = f32[128,256]{1,0:T(8,128)S(1)} collective-permute-done((f32[128,256]{1,0:T(8,128)S(1)}, f32[128,256]{1,0:T(8,128)S(1)}, u32[]{:S(2)}, u32[]{:S(2)}) %collective-permute-start.9) | collective-permute-done | bytes 131104 | tf_op jit(solution)/shard_map/ppermute | solution.py:345
  45.9 3.4 %collective-permute-done.8 = f32[128,256]{1,0:T(8,128)S(1)} collective-permute-done((f32[128,256]{1,0:T(8,128)S(1)}, f32[128,256]{1,0:T(8,128)S(1)}, u32[]{:S(2)}, u32[]{:S(2)}) %collective-permute-start.8) | collective-permute-done | bytes 131104 | tf_op jit(solution)/shard_map/ppermute | solution.py:345
  49.4 5.7 %collective-permute-start.11 = (f32[128,256]{1,0:T(8,128)S(1)}, f32[128,256]{1,0:T(8,128)S(1)}, u32[]{:S(2)}, u32[]{:S(2)}) collective-permute-start(f32[128,256]{1,0:T(8,128)S(1)} %add_add_fusion), channel_id=1, source_target_pairs={{0,32},{1,33},{2,34},{3,35},{4,36},{5,37},{6,38},{7,39},{8,40},{9,... | collective-permute-start | bytes 393224 | tf_op jit(solution)/shard_map/ppermute | solution.py:345
  55.1 2.4 %collective-permute-done.11 = f32[128,256]{1,0:T(8,128)S(1)} collective-permute-done((f32[128,256]{1,0:T(8,128)S(1)}, f32[128,256]{1,0:T(8,128)S(1)}, u32[]{:S(2)}, u32[]{:S(2)}) %collective-permute-start.11) | collective-permute-done | bytes 131104 | tf_op jit(solution)/shard_map/ppermute | solution.py:345
  57.5 3.3 %collective-permute-start.12 = (f32[128,256]{1,0:T(8,128)S(1)}, f32[128,256]{1,0:T(8,128)S(1)}, u32[]{:S(2)}, u32[]{:S(2)}) collective-permute-start(f32[128,256]{1,0:T(8,128)S(1)} %subtract_maximum_fusion), channel_id=1, source_target_pairs={{0,1},{1,0},{2,3},{3,2},{4,5},{5,4},{6,7},{7,6},{8,9},{9,8},{10,11... | collective-permute-start | bytes 393224 | tf_op jit(solution)/shard_map/ppermute | solution.py:348
  60.8 1.0 %collective-permute-done.12 = f32[128,256]{1,0:T(8,128)S(1)} collective-permute-done((f32[128,256]{1,0:T(8,128)S(1)}, f32[128,256]{1,0:T(8,128)S(1)}, u32[]{:S(2)}, u32[]{:S(2)}) %collective-permute-start.12) | collective-permute-done | bytes 131104 | tf_op jit(solution)/shard_map/ppermute | solution.py:348
  61.7 0.7 %maximum_select_fusion = f32[1,256,256]{2,1,0:T(8,128)} fusion(f32[1,128,256]{2,1,0:T(8,128)S(1)} %bitcast.12, f32[1,128,256]{2,1,0:T(8,128)S(1)} %bitcast.11, pred[]{:T(512)S(6)} %eq.5), kind=kLoop, calls=%fused_computation | loop fusion | flops 196608 | bytes 524289 | tf_op jit(solution)/shard_map/jit(_where)/select_n | solution.py:349
  (4 shorter events, 0.1 us)
Async XLA Ops:
  0.0 4.7 %copy-start = (f32[4,2,256,256]{3,2,1,0:T(8,128)S(1)}, f32[4,2,256,256]{3,2,1,0:T(8,128)}, u32[]{:S(2)}) copy-start(f32[4,2,256,256]{3,2,1,0:T(8,128)} %dual.1) | copy-start | bytes 6291460
  0.0 4.7 %copy-start.3 = (f32[256,256]{1,0:T(8,128)S(1)}, f32[256,256]{1,0:T(8,128)}, u32[]{:S(2)}) copy-start(f32[256,256]{1,0:T(8,128)} %phase.1) | copy-start | bytes 786436
  0.0 12.7 %collective-permute-start = (f32[256,256]{1,0:T(8,128)}, f32[256,256]{1,0:T(8,128)S(1)}, u32[]{:S(2)}, u32[]{:S(2)}) collective-permute-start(f32[256,256]{1,0:T(8,128)} %bitcast.9), channel_id=1, source_target_pairs={{192,32},{194,34},{196,36},{198,38},{200,40},{202,42},{204,44},{20... | collective-permute-start | bytes 786440 | tf_op jit(solution)/shard_map/ppermute | solution.py:297
  2.4 7.4 %collective-permute-start.1 = (f32[128,256]{1,0:T(8,128)S(1)}, f32[128,256]{1,0:T(8,128)S(1)}, u32[]{:S(2)}, u32[]{:S(2)}) collective-permute-start(f32[128,256]{1,0:T(8,128)S(1)} %dynamic-slice_bitcast_fusion), channel_id=1, source_target_pairs={{64,0},{66,2},{68,4},{70,6},{72,8},{74,10},{76,12},{78,14},{80,16}... | collective-permute-start | bytes 393224 | tf_op jit(solution)/shard_map/ppermute | solution.py:303
  4.7 11.9 %copy-start.1 = (f32[1,4,2,256,256]{4,3,2,1,0:T(8,128)S(1)}, f32[1,4,2,256,256]{4,3,2,1,0:T(8,128)}, u32[]{:S(2)}) copy-start(f32[1,4,2,256,256]{4,3,2,1,0:T(8,128)} %param.6) | copy-start | bytes 6291460
  4.8 11.9 %copy-start.2 = (f32[1,256,256]{2,1,0:T(8,128)S(1)}, f32[1,256,256]{2,1,0:T(8,128)}, u32[]{:S(2)}) copy-start(f32[1,256,256]{2,1,0:T(8,128)} %param.4) | copy-start | bytes 786436
  12.7 3.9 %collective-permute-start.2 = (f32[256,256]{1,0:T(8,128)S(1)}, f32[256,256]{1,0:T(8,128)S(1)}, u32[]{:S(2)}, u32[]{:S(2)}) collective-permute-start(f32[256,256]{1,0:T(8,128)S(1)} %collective-permute-done.got), channel_id=1, source_target_pairs={{0,1},{1,0},{2,3},{3,2},{4,5},{5,4},{6,7},{7,6},{8,9},{9,8},{10,11... | collective-permute-start | bytes 786440 | tf_op jit(solution)/shard_map/ppermute | solution.py:320
  15.3 1.3 %collective-permute-start.3 = (f32[128,256]{1,0:T(8,128)S(1)}, f32[128,256]{1,0:T(8,128)S(1)}, u32[]{:S(2)}, u32[]{:S(2)}) collective-permute-start(f32[128,256]{1,0:T(8,128)S(1)} %collective-permute-done.1.near), channel_id=1, source_target_pairs={{0,1},{1,0},{2,3},{3,2},{4,5},{5,4},{6,7},{7,6},{8,9},{9,8},{10,11... | collective-permute-start | bytes 393224 | tf_op jit(solution)/shard_map/ppermute | solution.py:321
  28.1 1.6 %collective-permute-start.4 = (f32[128,256]{1,0:T(8,128)S(1)}, f32[128,256]{1,0:T(8,128)S(1)}, u32[]{:S(2)}, u32[]{:S(2)}) collective-permute-start(f32[128,256]{1,0:T(8,128)S(1)} %get-tuple-element.20), channel_id=1, source_target_pairs={{0,1},{1,0},{2,3},{3,2},{4,5},{5,4},{6,7},{7,6},{8,9},{9,8},{10,11... | collective-permute-start | bytes 393224 | tf_op jit(solution)/shard_map/ppermute | solution.py:331
  29.8 4.8 %collective-permute-start.7 = (f32[128,256]{1,0:T(8,128)S(1)}, f32[128,256]{1,0:T(8,128)S(1)}, u32[]{:S(2)}, u32[]{:S(2)}) collective-permute-start(f32[128,256]{1,0:T(8,128)S(1)} %add.33), channel_id=1, source_target_pairs={{0,2},{1,3},{2,0},{3,1},{4,6},{5,7},{6,4},{7,5},{8,10},{9,11},{10,... | collective-permute-start | bytes 393224 | tf_op jit(solution)/shard_map/ppermute | solution.py:345
  31.1 6.7 %collective-permute-start.6 = (f32[128,256]{1,0:T(8,128)S(1)}, f32[128,256]{1,0:T(8,128)S(1)}, u32[]{:S(2)}, u32[]{:S(2)}) collective-permute-start(f32[128,256]{1,0:T(8,128)S(1)} %add.33), channel_id=1, source_target_pairs={{0,6},{1,7},{2,4},{3,5},{4,2},{5,3},{6,0},{7,1},{8,14},{9,15},{10,... | collective-permute-start | bytes 393224 | tf_op jit(solution)/shard_map/ppermute | solution.py:345
  32.9 6.6 %collective-permute-start.5 = (f32[128,256]{1,0:T(8,128)S(1)}, f32[128,256]{1,0:T(8,128)S(1)}, u32[]{:S(2)}, u32[]{:S(2)}) collective-permute-start(f32[128,256]{1,0:T(8,128)S(1)} %add.33), channel_id=1, source_target_pairs={{0,4},{1,5},{2,6},{3,7},{4,0},{5,1},{6,2},{7,3},{8,12},{9,13},{10,... | collective-permute-start | bytes 393224 | tf_op jit(solution)/shard_map/ppermute | solution.py:345
  39.5 4.0 %collective-permute-start.10 = (f32[128,256]{1,0:T(8,128)S(1)}, f32[128,256]{1,0:T(8,128)S(1)}, u32[]{:S(2)}, u32[]{:S(2)}) collective-permute-start(f32[128,256]{1,0:T(8,128)S(1)} %add_add_fusion.1), channel_id=1, source_target_pairs={{0,8},{1,9},{2,10},{3,11},{4,12},{5,13},{6,14},{7,15},{8,0},{9,1},... | collective-permute-start | bytes 393224 | tf_op jit(solution)/shard_map/ppermute | solution.py:345
  40.9 5.0 %collective-permute-start.9 = (f32[128,256]{1,0:T(8,128)S(1)}, f32[128,256]{1,0:T(8,128)S(1)}, u32[]{:S(2)}, u32[]{:S(2)}) collective-permute-start(f32[128,256]{1,0:T(8,128)S(1)} %add_add_fusion.1), channel_id=1, source_target_pairs={{0,24},{1,25},{2,26},{3,27},{4,28},{5,29},{6,30},{7,31},{8,16},{9,... | collective-permute-start | bytes 393224 | tf_op jit(solution)/shard_map/ppermute | solution.py:345
  42.8 6.6 %collective-permute-start.8 = (f32[128,256]{1,0:T(8,128)S(1)}, f32[128,256]{1,0:T(8,128)S(1)}, u32[]{:S(2)}, u32[]{:S(2)}) collective-permute-start(f32[128,256]{1,0:T(8,128)S(1)} %add_add_fusion.1), channel_id=1, source_target_pairs={{0,16},{1,17},{2,18},{3,19},{4,20},{5,21},{6,22},{7,23},{8,24},{9,... | collective-permute-start | bytes 393224 | tf_op jit(solution)/shard_map/ppermute | solution.py:345
  49.4 8.1 %collective-permute-start.11 = (f32[128,256]{1,0:T(8,128)S(1)}, f32[128,256]{1,0:T(8,128)S(1)}, u32[]{:S(2)}, u32[]{:S(2)}) collective-permute-start(f32[128,256]{1,0:T(8,128)S(1)} %add_add_fusion), channel_id=1, source_target_pairs={{0,32},{1,33},{2,34},{3,35},{4,36},{5,37},{6,38},{7,39},{8,40},{9,... | collective-permute-start | bytes 393224 | tf_op jit(solution)/shard_map/ppermute | solution.py:345
  57.5 4.2 %collective-permute-start.12 = (f32[128,256]{1,0:T(8,128)S(1)}, f32[128,256]{1,0:T(8,128)S(1)}, u32[]{:S(2)}, u32[]{:S(2)}) collective-permute-start(f32[128,256]{1,0:T(8,128)S(1)} %subtract_maximum_fusion), channel_id=1, source_target_pairs={{0,1},{1,0},{2,3},{3,2},{4,5},{5,4},{6,7},{7,6},{8,9},{9,8},{10,11... | collective-permute-start | bytes 393224 | tf_op jit(solution)/shard_map/ppermute | solution.py:348

commit v4 on v3

--- a/solution.py
+++ b/solution.py
@@ -149,14 +149,14 @@
     return c, s * turn
 
 
-def start_all(pairs, sems):
-    copies = [pltpu.make_async_copy(a, b, sems.at[n]) for n, (a, b) in enumerate(pairs)]
-    for copy in copies:
-        copy.start()
-    return copies
-
-
-def first_kernel(dual, phase, tabs, mu, h_same, h_cross, lanes):
+def set_t(plane, tr, ti, at=slice(None)):
+    c, s = half_range_cos_sin(PHASE_GAIN * plane[...])
+    tr[at, :] = c
+    ti[at, :] = s
+
+
+def first_kernel(dual, phase, tabs, own, mu, h_same, h_cross, own_tr, own_ti, lanes):
+    set_t(own, own_tr, own_ti)
     row = lax.broadcasted_iota(jnp.int32, (256, 128), 0)
     lane = lax.broadcasted_iota(jnp.int32, (256, 128), 1)
     col = lane % 64 * 4
@@ -195,55 +195,51 @@
 
 
 def rest_kernel(
-    mu_in, entry_in, h_same, h_cross, tabs, own, got, swapped, near, near_swapped,
-    keep, send, mu, entry, tr, ti, sems,
+    mu_in, entry, h_same, h_cross, tabs, own_tr, own_ti, got, swapped, near, near_swapped,
+    keep, send, mu, tr, ti,
 ):
     count = mu.shape[0]
-    mu_copy, entry_copy = start_all(((mu_in, mu), (entry_in, entry)), sems)
     left = 3 - lax.axis_index("gz")
     core = lax.axis_index("angle") % 2
-
-    def set_t(ref, at=slice(None)):
-        c, s = half_range_cos_sin(PHASE_GAIN * ref[...])
-        tr[at, :] = c
-        ti[at, :] = s
 
     def set_t_for(step):
         one_above = (left != 2) & (left - step == 1)
         here = (step % 2) == core
-        pl.when(~one_above & here)(lambda: set_t(got))
-        pl.when(~one_above & ~here)(lambda: set_t(swapped))
+        pl.when(~one_above & here)(lambda: set_t(got, tr, ti))
+        pl.when(~one_above & ~here)(lambda: set_t(swapped, tr, ti))
 
         @pl.when(one_above)
         def _():
-            set_t(near, pl.ds(pl.multiple_of(core * 128, 128), 128))
-            set_t(near_swapped, pl.ds(pl.multiple_of(128 - core * 128, 128), 128))
-
-    def load_from(angle):
+            set_t(near, tr, ti, pl.ds(pl.multiple_of(core * 128, 128), 128))
+            set_t(near_swapped, tr, ti, pl.ds(pl.multiple_of(128 - core * 128, 128), 128))
+
+    def load_from(ref, angle):
         def load(p):
             at = quarter_at(p)
-            r, i = mu[angle, 0, at, :], mu[angle, 1, at, :]
+            r, i = ref[angle, 0, at, :], ref[angle, 1, at, :]
             return tr[at, :] * r + ti[at, :] * i, tr[at, :] * i - ti[at, :] * r
 
         return load
 
-    set_t_for(0)
-    mu_copy.wait()
-
-    def one_slab(step, carry):
-        pl.when(step > 0)(lambda: set_t_for(step))
+    def one_slab(step, ref):
+        set_t_for(step)
         adjoint_step(
-            [load_from(n) for n in range(count)],
+            [load_from(ref, n) for n in range(count)],
             [store_into(mu, n) for n in range(count)],
             tabs,
             h_same,
             h_cross,
         )
-        return carry
-
-    lax.fori_loop(0, left, one_slab, 0)
-    set_t(own)
-    entry_copy.wait()
+
+    @pl.when(left > 0)
+    def _():
+        one_slab(0, mu_in)
+
+    @pl.when(left == 0)
+    def _():
+        mu[...] = mu_in[...]
+
+    lax.fori_loop(1, left, lambda step, _: one_slab(step, mu), None)
 
     def terms(at):
         gr = gi = 0.0
@@ -252,7 +248,7 @@
             er, ei = entry[n, 0, at, :], entry[n, 1, at, :]
             gr += r * er + i * ei
             gi += i * er - r * ei
-        return PHASE_GAIN * (tr[at, :] * gi - ti[at, :] * gr)
+        return PHASE_GAIN * (own_tr[at, :] * gi - own_ti[at, :] * gr)
 
     for at in range(0, 128, 32):
         keep[pl.ds(at, 32), :] = terms(pl.ds(pl.multiple_of(core * 128 + at, 32), 32))
@@ -310,12 +306,12 @@
     tabs = call(
         tables_kernel, (), jax.ShapeDtypeStruct((4, 4, 256, 256), jnp.bfloat16), ()
     )()
-    mu, h_same, h_cross = call(
+    mu, h_same, h_cross, own_tr, own_ti = call(
         first_kernel,
-        (False,) * 3,
-        (f32(*field), f32(*h_shape), f32(*h_shape)),
+        (False,) * 4,
+        (f32(*field), f32(*h_shape), f32(*h_shape), f32(256, 256), f32(256, 256)),
         [pltpu.VMEM((512, 128), jnp.float32)],
-    )(exit_cotangent, prop_phase, tabs)
+    )(exit_cotangent, prop_phase, tabs, own)
     got, near, mu = lax.optimization_barrier((got, near, mu))
     swapped = lax.ppermute(got, "angle", swap)
     near_swapped = lax.ppermute(near, "angle", swap)
@@ -323,22 +319,25 @@
     plane = pltpu.VMEM((256, 256), jnp.float32)
     keep, send = call(
         rest_kernel,
-        (True,) * 2 + (False,) * 8,
+        (False,) * 11,
         (f32(128, 256), f32(128, 256)),
-        [fields, fields, plane, plane, pltpu.SemaphoreType.DMA((2,))],
-    )(mu, entry_field[0], h_same, h_cross, tabs, own, got, swapped, near, near_swapped)
+        [fields, plane, plane],
+    )(
+        mu, entry_field[0], h_same, h_cross, tabs, own_tr, own_ti,
+        got, swapped, near, near_swapped,
+    )
 
     total = keep + lax.ppermute(send, "angle", swap)
     for ring in (
         (
             lambda z, y, x, c: (z, y, x ^ 2, c),
+            lambda z, y, x, c: (z, y, x ^ 1, c),
             lambda z, y, x, c: (z, y, 3 - x, c),
-            lambda z, y, x, c: (z, y, x ^ 1, c),
         ),
         (
             lambda z, y, x, c: (z, y ^ 2, x, c),
+            lambda z, y, x, c: (z, y ^ 1, x, c),
             lambda z, y, x, c: (z, 3 - y, x, c),
-            lambda z, y, x, c: (z, y ^ 1, x, c),
         ),
         (lambda z, y, x, c: (1 - z, y, x, c),),
     ):

time: 62.6 us -> 61.6 us (0.984)
  waiting for transfers between devices: 21.7 us -> 19.8 us
  local copies, waits for them, and re-layouts: 0.94 us -> 1.87 us
    ppermute x1, waiting for transfers between devices: 1.19 us -> 0.01 us  [per_device(): lax.ppermute(mine, ('gz', 'angle'), slab_pairs(((1, 0, 0, 0, 0), (1, 1, 0...]
    unnamed x8, local copies, waits for them, and re-layouts: 0.02 us -> 0.96 us
where the time goes in v4:
time: 61.6 us; the launch traced here: 61.4 us
  starting transfers between devices  22.5 us (37%)
  waiting for transfers between devices  19.8 us (32%)
  Pallas kernels  16.3 us (26%)
  local copies, waits for them, and re-layouts  1.87 us (3%)
  other arithmetic  0.84 us (1%)
    ppermute x7, starting transfers between devices, per_device(): lax.ppermute(total, 'angle', angle_pairs(p))  13.8 us
    ppermute x7, waiting for transfers between devices, per_device(): lax.ppermute(total, 'angle', angle_pairs(p))  13.6 us
    pallas_call x1, Pallas kernels, per_device(): call(rest_kernel, (False,) * 11, (f32(128, 256), f32(128, 256)), [fields,...  11.1 us
    pallas_call x1, Pallas kernels, per_device(): call(first_kernel, (False,) * 4, (f32(*field), f32(*h_shape), f32(*h_shap...  4.12 us
    ppermute x1, starting transfers between devices, per_device(): other = lax.ppermute(new, 'angle', swap)  3.02 us
    ppermute x1, waiting for transfers between devices, per_device(): lax.ppermute(own, ('gz', 'angle'), slab_pairs(((3, 0, 0, 0, 1), (2, 0, 0,...  2.9 us
    ppermute x1, starting transfers between devices, per_device(): swapped = lax.ppermute(got, 'angle', swap)  2.54 us
    ppermute x1, starting transfers between devices, per_device(): lax.ppermute(own, ('gz', 'angle'), slab_pairs(((3, 0, 0, 0, 1), (2, 0, 0,...  1.41 us
  transfers between devices with their start and end apart: 13, of which 11 were waited for; matrix products, arithmetic and copies ran while one was open for 1% of the time, Pallas kernels for 8%

profile of v4, /device:TPU:1, one launch (start us, length us, event | category | flops | bytes accessed | tf_op | source)
XLA Modules:
  0.0 61.4 jit_solution(14198171376166941569)
XLA Ops:
  0.0 0.0 copy-start.2
  0.0 0.0 copy-start
  0.0 1.4 %collective-permute-start = (f32[256,256]{1,0:T(8,128)}, f32[256,256]{1,0:T(8,128)S(1)}, u32[]{:S(2)}, u32[]{:S(2)}) collective-permute-start(f32[256,256]{1,0:T(8,128)} %bitcast.9), channel_id=1, source_target_pairs={{192,32},{194,34},{196,36},{198,38},{200,40},{202,42},{204,44},{20... | collective-permute-start | bytes 786440 | tf_op jit(solution)/shard_map/ppermute | solution.py:293
  1.4 0.9 %dynamic-slice_bitcast_fusion = f32[128,256]{1,0:T(8,128)S(1)} fusion(f32[1,256,256]{2,1,0:T(8,128)} %param.4, s32[]{:T(128)S(6)} %select_n.27), kind=kLoop, calls=%fused_computation.4 | loop fusion | bytes 262148 | tf_op jit(solution)/shard_map/dynamic_slice | solution.py:298
  2.4 1.3 %collective-permute-start.1 = (f32[128,256]{1,0:T(8,128)S(1)}, f32[128,256]{1,0:T(8,128)S(1)}, u32[]{:S(2)}, u32[]{:S(2)}) collective-permute-start(f32[128,256]{1,0:T(8,128)S(1)} %dynamic-slice_bitcast_fusion), channel_id=1, source_target_pairs={{64,0},{66,2},{68,4},{70,6},{72,8},{74,10},{76,12},{78,14},{80,16}... | collective-permute-start | bytes 393224 | tf_op jit(solution)/shard_map/ppermute | solution.py:299
  3.7 1.1 %shard_map.46.tabs = bf16[4,4,256,256]{3,2,1,0:T(8,128)(2,1)S(1)} custom-call(), custom_call_target="tpu_custom_call" | custom-call | tf_op jit(solution)/shard_map/pallas_call | solution.py:306
  4.7 0.0 copy-done.2
  4.7 0.0 copy-done
  4.7 0.0 copy-start.3
  4.8 0.9 %copy-done.3 = f32[256,256]{1,0:T(8,128)S(1)} copy-done((f32[256,256]{1,0:T(8,128)S(1)}, f32[256,256]{1,0:T(8,128)}, u32[]{:S(2)}) %copy-start.3) | copy-done | bytes 262168
  5.7 0.0 copy-start.1
  5.7 4.1 %shard_map.47 = (f32[4,2,256,256]{3,2,1,0:T(8,128)S(1)}, f32[4,256,128]{2,1,0:T(8,128)S(1)}, f32[4,256,128]{2,1,0:T(8,128)S(1)}, f32[256,256]{1,0:T(8,128)S(1)}, f32[256,256]{1,0:T(8,128)S(1)}) custom-call(f32[4,2,256,256]{3,2,1,0:T(8,128)S(1)} %copy-done, f32[256,256]{1,0:T(8,128)S(1)} %copy-done.3, bf16[4,4,256,256]{3,2,1,0:T(8,128)(2,1)S(1)} %shard_map.46.tabs, ...), custom_call_target="tpu_custom_call" | custom-call | tf_op jit(solution)/shard_map/pallas_call | solution.py:309
  9.8 0.0 collective-permute-done.1.near
  9.8 2.9 %collective-permute-done.got = f32[256,256]{1,0:T(8,128)S(1)} collective-permute-done((f32[256,256]{1,0:T(8,128)}, f32[256,256]{1,0:T(8,128)S(1)}, u32[]{:S(2)}, u32[]{:S(2)}) %collective-permute-start) | collective-permute-done | bytes 262176 | tf_op jit(solution)/shard_map/ppermute | solution.py:293
  12.7 2.5 %collective-permute-start.2 = (f32[256,256]{1,0:T(8,128)S(1)}, f32[256,256]{1,0:T(8,128)S(1)}, u32[]{:S(2)}, u32[]{:S(2)}) collective-permute-start(f32[256,256]{1,0:T(8,128)S(1)} %collective-permute-done.got), channel_id=1, source_target_pairs={{0,1},{1,0},{2,3},{3,2},{4,5},{5,4},{6,7},{7,6},{8,9},{9,8},{10,11... | collective-permute-start | bytes 786440 | tf_op jit(solution)/shard_map/ppermute | solution.py:316
  15.3 0.0 collective-permute-start.3
  15.3 1.3 %collective-permute-done.3.near_swapped = f32[128,256]{1,0:T(8,128)S(1)} collective-permute-done((f32[128,256]{1,0:T(8,128)S(1)}, f32[128,256]{1,0:T(8,128)S(1)}, u32[]{:S(2)}, u32[]{:S(2)}) %collective-permute-start.3) | collective-permute-done | bytes 131104 | tf_op jit(solution)/shard_map/ppermute | solution.py:317
  16.6 0.0 collective-permute-done.2.swapped
  16.6 0.0 copy-done.1
  16.6 11.1 %shard_map.48 = (f32[128,256]{1,0:T(8,128)S(1)}, f32[128,256]{1,0:T(8,128)S(1)}) custom-call(f32[4,2,256,256]{3,2,1,0:T(8,128)S(1)} %get-tuple-element.16.mu_in, f32[4,2,256,256]{3,2,1,0:T(8,128)S(1)} %bitcast.8, f32[4,256,128]{2,1,0:T(8,128)S(1)} %get-tuple-element.17.h_same, f32[4,256,128]{2,1,0:T(8,128)S(1)} %get-tuple-element.18.h_cross, ...), custom_call_target="tpu_custom_call" | custom-call | tf_op jit(solution)/shard_map/pallas_call | solution.py:320
  27.7 0.5 collective-permute-start.4
  28.2 1.0 %collective-permute-done.4 = f32[128,256]{1,0:T(8,128)S(1)} collective-permute-done((f32[128,256]{1,0:T(8,128)S(1)}, f32[128,256]{1,0:T(8,128)S(1)}, u32[]{:S(2)}, u32[]{:S(2)}) %collective-permute-start.4) | collective-permute-done | bytes 131104 | tf_op jit(solution)/shard_map/ppermute | solution.py:330
  29.2 2.6 %collective-permute-start.7 = (f32[128,256]{1,0:T(8,128)S(1)}, f32[128,256]{1,0:T(8,128)S(1)}, u32[]{:S(2)}, u32[]{:S(2)}) collective-permute-start(f32[128,256]{1,0:T(8,128)S(1)} %add.33), channel_id=1, source_target_pairs={{0,6},{1,7},{2,4},{3,5},{4,2},{5,3},{6,0},{7,1},{8,14},{9,15},{10,... | collective-permute-start | bytes 393224 | tf_op jit(solution)/shard_map/ppermute | solution.py:344
  31.8 0.0 collective-permute-start.6
  31.8 1.4 %collective-permute-start.5 = (f32[128,256]{1,0:T(8,128)S(1)}, f32[128,256]{1,0:T(8,128)S(1)}, u32[]{:S(2)}, u32[]{:S(2)}) collective-permute-start(f32[128,256]{1,0:T(8,128)S(1)} %add.33), channel_id=1, source_target_pairs={{0,4},{1,5},{2,6},{3,7},{4,0},{5,1},{6,2},{7,3},{8,12},{9,13},{10,... | collective-permute-start | bytes 393224 | tf_op jit(solution)/shard_map/ppermute | solution.py:344
  33.1 2.1 %collective-permute-done.7 = f32[128,256]{1,0:T(8,128)S(1)} collective-permute-done((f32[128,256]{1,0:T(8,128)S(1)}, f32[128,256]{1,0:T(8,128)S(1)}, u32[]{:S(2)}, u32[]{:S(2)}) %collective-permute-start.7) | collective-permute-done | bytes 131104 | tf_op jit(solution)/shard_map/ppermute | solution.py:344
  35.2 1.0 %collective-permute-done.6 = f32[128,256]{1,0:T(8,128)S(1)} collective-permute-done((f32[128,256]{1,0:T(8,128)S(1)}, f32[128,256]{1,0:T(8,128)S(1)}, u32[]{:S(2)}, u32[]{:S(2)}) %collective-permute-start.6) | collective-permute-done | bytes 131104 | tf_op jit(solution)/shard_map/ppermute | solution.py:344
  36.2 2.7 %collective-permute-done.5 = f32[128,256]{1,0:T(8,128)S(1)} collective-permute-done((f32[128,256]{1,0:T(8,128)S(1)}, f32[128,256]{1,0:T(8,128)S(1)}, u32[]{:S(2)}, u32[]{:S(2)}) %collective-permute-start.5) | collective-permute-done | bytes 131104 | tf_op jit(solution)/shard_map/ppermute | solution.py:344
  38.9 2.8 %collective-permute-start.10 = (f32[128,256]{1,0:T(8,128)S(1)}, f32[128,256]{1,0:T(8,128)S(1)}, u32[]{:S(2)}, u32[]{:S(2)}) collective-permute-start(f32[128,256]{1,0:T(8,128)S(1)} %add_add_fusion.1), channel_id=1, source_target_pairs={{0,24},{1,25},{2,26},{3,27},{4,28},{5,29},{6,30},{7,31},{8,16},{9,... | collective-permute-start | bytes 393224 | tf_op jit(solution)/shard_map/ppermute | solution.py:344
  41.7 0.0 collective-permute-start.9
  41.7 1.3 %collective-permute-start.8 = (f32[128,256]{1,0:T(8,128)S(1)}, f32[128,256]{1,0:T(8,128)S(1)}, u32[]{:S(2)}, u32[]{:S(2)}) collective-permute-start(f32[128,256]{1,0:T(8,128)S(1)} %add_add_fusion.1), channel_id=1, source_target_pairs={{0,16},{1,17},{2,18},{3,19},{4,20},{5,21},{6,22},{7,23},{8,24},{9,... | collective-permute-start | bytes 393224 | tf_op jit(solution)/shard_map/ppermute | solution.py:344
  43.0 1.1 %collective-permute-done.10 = f32[128,256]{1,0:T(8,128)S(1)} collective-permute-done((f32[128,256]{1,0:T(8,128)S(1)}, f32[128,256]{1,0:T(8,128)S(1)}, u32[]{:S(2)}, u32[]{:S(2)}) %collective-permute-start.10) | collective-permute-done | bytes 131104 | tf_op jit(solution)/shard_map/ppermute | solution.py:344
  44.1 1.8 %collective-permute-done.9 = f32[128,256]{1,0:T(8,128)S(1)} collective-permute-done((f32[128,256]{1,0:T(8,128)S(1)}, f32[128,256]{1,0:T(8,128)S(1)}, u32[]{:S(2)}, u32[]{:S(2)}) %collective-permute-start.9) | collective-permute-done | bytes 131104 | tf_op jit(solution)/shard_map/ppermute | solution.py:344
  45.9 2.3 %collective-permute-done.8 = f32[128,256]{1,0:T(8,128)S(1)} collective-permute-done((f32[128,256]{1,0:T(8,128)S(1)}, f32[128,256]{1,0:T(8,128)S(1)}, u32[]{:S(2)}, u32[]{:S(2)}) %collective-permute-start.8) | collective-permute-done | bytes 131104 | tf_op jit(solution)/shard_map/ppermute | solution.py:344
  48.2 5.7 %collective-permute-start.11 = (f32[128,256]{1,0:T(8,128)S(1)}, f32[128,256]{1,0:T(8,128)S(1)}, u32[]{:S(2)}, u32[]{:S(2)}) collective-permute-start(f32[128,256]{1,0:T(8,128)S(1)} %add_add_fusion), channel_id=1, source_target_pairs={{0,32},{1,33},{2,34},{3,35},{4,36},{5,37},{6,38},{7,39},{8,40},{9,... | collective-permute-start | bytes 393224 | tf_op jit(solution)/shard_map/ppermute | solution.py:344
  53.9 2.7 %collective-permute-done.11 = f32[128,256]{1,0:T(8,128)S(1)} collective-permute-done((f32[128,256]{1,0:T(8,128)S(1)}, f32[128,256]{1,0:T(8,128)S(1)}, u32[]{:S(2)}, u32[]{:S(2)}) %collective-permute-start.11) | collective-permute-done | bytes 131104 | tf_op jit(solution)/shard_map/ppermute | solution.py:344
  56.7 3.0 %collective-permute-start.12 = (f32[128,256]{1,0:T(8,128)S(1)}, f32[128,256]{1,0:T(8,128)S(1)}, u32[]{:S(2)}, u32[]{:S(2)}) collective-permute-start(f32[128,256]{1,0:T(8,128)S(1)} %subtract_maximum_fusion), channel_id=1, source_target_pairs={{0,1},{1,0},{2,3},{3,2},{4,5},{5,4},{6,7},{7,6},{8,9},{9,8},{10,11... | collective-permute-start | bytes 393224 | tf_op jit(solution)/shard_map/ppermute | solution.py:347
  59.7 1.0 %collective-permute-done.12 = f32[128,256]{1,0:T(8,128)S(1)} collective-permute-done((f32[128,256]{1,0:T(8,128)S(1)}, f32[128,256]{1,0:T(8,128)S(1)}, u32[]{:S(2)}, u32[]{:S(2)}) %collective-permute-start.12) | collective-permute-done | bytes 131104 | tf_op jit(solution)/shard_map/ppermute | solution.py:347
  60.7 0.7 %maximum_select_fusion = f32[1,256,256]{2,1,0:T(8,128)} fusion(f32[1,128,256]{2,1,0:T(8,128)S(1)} %bitcast.12, f32[1,128,256]{2,1,0:T(8,128)S(1)} %bitcast.11, pred[]{:T(512)S(6)} %eq.5), kind=kLoop, calls=%fused_computation | loop fusion | flops 196608 | bytes 524289 | tf_op jit(solution)/shard_map/jit(_where)/select_n | solution.py:348
  (4 shorter events, 0.1 us)
Async XLA Ops:
  0.0 4.7 %copy-start.2 = (f32[1,256,256]{2,1,0:T(8,128)S(1)}, f32[1,256,256]{2,1,0:T(8,128)}, u32[]{:S(2)}) copy-start(f32[1,256,256]{2,1,0:T(8,128)} %param.4) | copy-start | bytes 786436
  0.0 4.7 %copy-start = (f32[4,2,256,256]{3,2,1,0:T(8,128)S(1)}, f32[4,2,256,256]{3,2,1,0:T(8,128)}, u32[]{:S(2)}) copy-start(f32[4,2,256,256]{3,2,1,0:T(8,128)} %dual.1) | copy-start | bytes 6291460
  0.0 12.7 %collective-permute-start = (f32[256,256]{1,0:T(8,128)}, f32[256,256]{1,0:T(8,128)S(1)}, u32[]{:S(2)}, u32[]{:S(2)}) collective-permute-start(f32[256,256]{1,0:T(8,128)} %bitcast.9), channel_id=1, source_target_pairs={{192,32},{194,34},{196,36},{198,38},{200,40},{202,42},{204,44},{20... | collective-permute-start | bytes 786440 | tf_op jit(solution)/shard_map/ppermute | solution.py:293
  2.4 7.5 %collective-permute-start.1 = (f32[128,256]{1,0:T(8,128)S(1)}, f32[128,256]{1,0:T(8,128)S(1)}, u32[]{:S(2)}, u32[]{:S(2)}) collective-permute-start(f32[128,256]{1,0:T(8,128)S(1)} %dynamic-slice_bitcast_fusion), channel_id=1, source_target_pairs={{64,0},{66,2},{68,4},{70,6},{72,8},{74,10},{76,12},{78,14},{80,16}... | collective-permute-start | bytes 393224 | tf_op jit(solution)/shard_map/ppermute | solution.py:299
  4.7 1.0 %copy-start.3 = (f32[256,256]{1,0:T(8,128)S(1)}, f32[256,256]{1,0:T(8,128)}, u32[]{:S(2)}) copy-start(f32[256,256]{1,0:T(8,128)} %phase.1) | copy-start | bytes 786436
  5.7 10.9 %copy-start.1 = (f32[1,4,2,256,256]{4,3,2,1,0:T(8,128)S(1)}, f32[1,4,2,256,256]{4,3,2,1,0:T(8,128)}, u32[]{:S(2)}) copy-start(f32[1,4,2,256,256]{4,3,2,1,0:T(8,128)} %param.6) | copy-start | bytes 6291460
  12.7 3.9 %collective-permute-start.2 = (f32[256,256]{1,0:T(8,128)S(1)}, f32[256,256]{1,0:T(8,128)S(1)}, u32[]{:S(2)}, u32[]{:S(2)}) collective-permute-start(f32[256,256]{1,0:T(8,128)S(1)} %collective-permute-done.got), channel_id=1, source_target_pairs={{0,1},{1,0},{2,3},{3,2},{4,5},{5,4},{6,7},{7,6},{8,9},{9,8},{10,11... | collective-permute-start | bytes 786440 | tf_op jit(solution)/shard_map/ppermute | solution.py:316
  15.3 1.3 %collective-permute-start.3 = (f32[128,256]{1,0:T(8,128)S(1)}, f32[128,256]{1,0:T(8,128)S(1)}, u32[]{:S(2)}, u32[]{:S(2)}) collective-permute-start(f32[128,256]{1,0:T(8,128)S(1)} %collective-permute-done.1.near), channel_id=1, source_target_pairs={{0,1},{1,0},{2,3},{3,2},{4,5},{5,4},{6,7},{7,6},{8,9},{9,8},{10,11... | collective-permute-start | bytes 393224 | tf_op jit(solution)/shard_map/ppermute | solution.py:317
  27.7 1.5 %collective-permute-start.4 = (f32[128,256]{1,0:T(8,128)S(1)}, f32[128,256]{1,0:T(8,128)S(1)}, u32[]{:S(2)}, u32[]{:S(2)}) collective-permute-start(f32[128,256]{1,0:T(8,128)S(1)} %get-tuple-element.24), channel_id=1, source_target_pairs={{0,1},{1,0},{2,3},{3,2},{4,5},{5,4},{6,7},{7,6},{8,9},{9,8},{10,11... | collective-permute-start | bytes 393224 | tf_op jit(solution)/shard_map/ppermute | solution.py:330
  29.2 6.0 %collective-permute-start.7 = (f32[128,256]{1,0:T(8,128)S(1)}, f32[128,256]{1,0:T(8,128)S(1)}, u32[]{:S(2)}, u32[]{:S(2)}) collective-permute-start(f32[128,256]{1,0:T(8,128)S(1)} %add.33), channel_id=1, source_target_pairs={{0,6},{1,7},{2,4},{3,5},{4,2},{5,3},{6,0},{7,1},{8,14},{9,15},{10,... | collective-permute-start | bytes 393224 | tf_op jit(solution)/shard_map/ppermute | solution.py:344
  31.8 4.4 %collective-permute-start.6 = (f32[128,256]{1,0:T(8,128)S(1)}, f32[128,256]{1,0:T(8,128)S(1)}, u32[]{:S(2)}, u32[]{:S(2)}) collective-permute-start(f32[128,256]{1,0:T(8,128)S(1)} %add.33), channel_id=1, source_target_pairs={{0,2},{1,3},{2,0},{3,1},{4,6},{5,7},{6,4},{7,5},{8,10},{9,11},{10,... | collective-permute-start | bytes 393224 | tf_op jit(solution)/shard_map/ppermute | solution.py:344
  31.8 7.1 %collective-permute-start.5 = (f32[128,256]{1,0:T(8,128)S(1)}, f32[128,256]{1,0:T(8,128)S(1)}, u32[]{:S(2)}, u32[]{:S(2)}) collective-permute-start(f32[128,256]{1,0:T(8,128)S(1)} %add.33), channel_id=1, source_target_pairs={{0,4},{1,5},{2,6},{3,7},{4,0},{5,1},{6,2},{7,3},{8,12},{9,13},{10,... | collective-permute-start | bytes 393224 | tf_op jit(solution)/shard_map/ppermute | solution.py:344
  38.9 5.2 %collective-permute-start.10 = (f32[128,256]{1,0:T(8,128)S(1)}, f32[128,256]{1,0:T(8,128)S(1)}, u32[]{:S(2)}, u32[]{:S(2)}) collective-permute-start(f32[128,256]{1,0:T(8,128)S(1)} %add_add_fusion.1), channel_id=1, source_target_pairs={{0,24},{1,25},{2,26},{3,27},{4,28},{5,29},{6,30},{7,31},{8,16},{9,... | collective-permute-start | bytes 393224 | tf_op jit(solution)/shard_map/ppermute | solution.py:344
  41.7 4.1 %collective-permute-start.9 = (f32[128,256]{1,0:T(8,128)S(1)}, f32[128,256]{1,0:T(8,128)S(1)}, u32[]{:S(2)}, u32[]{:S(2)}) collective-permute-start(f32[128,256]{1,0:T(8,128)S(1)} %add_add_fusion.1), channel_id=1, source_target_pairs={{0,8},{1,9},{2,10},{3,11},{4,12},{5,13},{6,14},{7,15},{8,0},{9,1},... | collective-permute-start | bytes 393224 | tf_op jit(solution)/shard_map/ppermute | solution.py:344
  41.7 6.4 %collective-permute-start.8 = (f32[128,256]{1,0:T(8,128)S(1)}, f32[128,256]{1,0:T(8,128)S(1)}, u32[]{:S(2)}, u32[]{:S(2)}) collective-permute-start(f32[128,256]{1,0:T(8,128)S(1)} %add_add_fusion.1), channel_id=1, source_target_pairs={{0,16},{1,17},{2,18},{3,19},{4,20},{5,21},{6,22},{7,23},{8,24},{9,... | collective-permute-start | bytes 393224 | tf_op jit(solution)/shard_map/ppermute | solution.py:344
  48.2 8.4 %collective-permute-start.11 = (f32[128,256]{1,0:T(8,128)S(1)}, f32[128,256]{1,0:T(8,128)S(1)}, u32[]{:S(2)}, u32[]{:S(2)}) collective-permute-start(f32[128,256]{1,0:T(8,128)S(1)} %add_add_fusion), channel_id=1, source_target_pairs={{0,32},{1,33},{2,34},{3,35},{4,36},{5,37},{6,38},{7,39},{8,40},{9,... | collective-permute-start | bytes 393224 | tf_op jit(solution)/shard_map/ppermute | solution.py:344
  56.7 4.0 %collective-permute-start.12 = (f32[128,256]{1,0:T(8,128)S(1)}, f32[128,256]{1,0:T(8,128)S(1)}, u32[]{:S(2)}, u32[]{:S(2)}) collective-permute-start(f32[128,256]{1,0:T(8,128)S(1)} %subtract_maximum_fusion), channel_id=1, source_target_pairs={{0,1},{1,0},{2,3},{3,2},{4,5},{5,4},{6,7},{7,6},{8,9},{9,8},{10,11... | collective-permute-start | bytes 393224 | tf_op jit(solution)/shard_map/ppermute | solution.py:347

commit v5 on v4

--- a/solution.py
+++ b/solution.py
@@ -293,7 +293,7 @@
     got = lax.ppermute(
         own,
         ("gz", "angle"),
-        slab_pairs(((3, 0, 0, 0, 1), (2, 0, 0, 1, 0), (3, 1, 1, 0, 1), (2, 1, 1, 1, 0))),
+        slab_pairs(((3, 0, 0, 0, 0), (2, 0, 0, 1, 1), (3, 1, 1, 0, 1), (2, 1, 1, 1, 0))),
     )
     mine = lax.dynamic_slice_in_dim(own, core * 128, 128, 0)
     near = lax.ppermute(

time: 61.6 us -> 61.6 us (level)
  starting transfers between devices: 22.5 us -> 21.4 us
  waiting for transfers between devices: 19.8 us -> 20.9 us
    ppermute x1, starting transfers between devices: 3.02 us -> 1.73 us  [per_device(): other = lax.ppermute(new, 'angle', swap)]
    ppermute x7, starting transfers between devices: 13.8 us -> 14.7 us  [per_device(): lax.ppermute(total, 'angle', angle_pairs(p))]
    ppermute x1, starting transfers between devices: 2.54 us -> 1.8 us  [per_device(): swapped = lax.ppermute(got, 'angle', swap)]
  transfers between devices with their start and end apart: 13 -> 13, of which waited for: 11 -> 10; matrix products, arithmetic and copies ran while one was open for 1% -> 1% of each run, Pallas kernels for 8% -> 8%
where the time goes in v5:
time: 61.6 us; the launch traced here: 61.4 us
  starting transfers between devices  21.4 us (35%)
  waiting for transfers between devices  20.9 us (34%)
  Pallas kernels  16.3 us (26%)
  local copies, waits for them, and re-layouts  1.87 us (3%)
  other arithmetic  0.84 us (1%)
    ppermute x7, starting transfers between devices, per_device(): lax.ppermute(total, 'angle', angle_pairs(p))  14.7 us
    ppermute x7, waiting for transfers between devices, per_device(): lax.ppermute(total, 'angle', angle_pairs(p))  14.2 us
    pallas_call x1, Pallas kernels, per_device(): call(rest_kernel, (False,) * 11, (f32(128, 256), f32(128, 256)), [fields,...  11.1 us
    pallas_call x1, Pallas kernels, per_device(): call(first_kernel, (False,) * 4, (f32(*field), f32(*h_shape), f32(*h_shap...  4.12 us
    ppermute x1, waiting for transfers between devices, per_device(): lax.ppermute(own, ('gz', 'angle'), slab_pairs(((3, 0, 0, 0, 0), (2, 0, 0,...  3.41 us
    ppermute x1, starting transfers between devices, per_device(): swapped = lax.ppermute(got, 'angle', swap)  1.8 us
    ppermute x1, starting transfers between devices, per_device(): other = lax.ppermute(new, 'angle', swap)  1.73 us
    ppermute x1, starting transfers between devices, per_device(): lax.ppermute(own, ('gz', 'angle'), slab_pairs(((3, 0, 0, 0, 0), (2, 0, 0,...  1.41 us
  transfers between devices with their start and end apart: 13, of which 10 were waited for; matrix products, arithmetic and copies ran while one was open for 1% of the time, Pallas kernels for 8%

profile of v5, /device:TPU:1, one launch (start us, length us, event | category | flops | bytes accessed | tf_op | source)
XLA Modules:
  0.0 61.4 jit_solution(2377606911314539354)
XLA Ops:
  0.0 0.0 copy-start.2
  0.0 0.0 copy-start
  0.0 1.4 %collective-permute-start = (f32[256,256]{1,0:T(8,128)}, f32[256,256]{1,0:T(8,128)S(1)}, u32[]{:S(2)}, u32[]{:S(2)}) collective-permute-start(f32[256,256]{1,0:T(8,128)} %bitcast.9), channel_id=1, source_target_pairs={{192,0},{194,2},{196,4},{198,6},{200,8},{202,10},{204,12},{206,14}... | collective-permute-start | bytes 786440 | tf_op jit(solution)/shard_map/ppermute | solution.py:293
  1.4 0.9 %dynamic-slice_bitcast_fusion = f32[128,256]{1,0:T(8,128)S(1)} fusion(f32[1,256,256]{2,1,0:T(8,128)} %param.4, s32[]{:T(128)S(6)} %select_n.27), kind=kLoop, calls=%fused_computation.4 | loop fusion | bytes 262148 | tf_op jit(solution)/shard_map/dynamic_slice | solution.py:298
  2.4 1.3 %collective-permute-start.1 = (f32[128,256]{1,0:T(8,128)S(1)}, f32[128,256]{1,0:T(8,128)S(1)}, u32[]{:S(2)}, u32[]{:S(2)}) collective-permute-start(f32[128,256]{1,0:T(8,128)S(1)} %dynamic-slice_bitcast_fusion), channel_id=1, source_target_pairs={{64,0},{66,2},{68,4},{70,6},{72,8},{74,10},{76,12},{78,14},{80,16}... | collective-permute-start | bytes 393224 | tf_op jit(solution)/shard_map/ppermute | solution.py:299
  3.7 1.1 %shard_map.46.tabs = bf16[4,4,256,256]{3,2,1,0:T(8,128)(2,1)S(1)} custom-call(), custom_call_target="tpu_custom_call" | custom-call | tf_op jit(solution)/shard_map/pallas_call | solution.py:306
  4.7 0.0 copy-done.2
  4.7 0.0 copy-done
  4.7 0.0 copy-start.3
  4.8 0.9 %copy-done.3 = f32[256,256]{1,0:T(8,128)S(1)} copy-done((f32[256,256]{1,0:T(8,128)S(1)}, f32[256,256]{1,0:T(8,128)}, u32[]{:S(2)}) %copy-start.3) | copy-done | bytes 262168
  5.7 0.0 copy-start.1
  5.7 4.1 %shard_map.47 = (f32[4,2,256,256]{3,2,1,0:T(8,128)S(1)}, f32[4,256,128]{2,1,0:T(8,128)S(1)}, f32[4,256,128]{2,1,0:T(8,128)S(1)}, f32[256,256]{1,0:T(8,128)S(1)}, f32[256,256]{1,0:T(8,128)S(1)}) custom-call(f32[4,2,256,256]{3,2,1,0:T(8,128)S(1)} %copy-done, f32[256,256]{1,0:T(8,128)S(1)} %copy-done.3, bf16[4,4,256,256]{3,2,1,0:T(8,128)(2,1)S(1)} %shard_map.46.tabs, ...), custom_call_target="tpu_custom_call" | custom-call | tf_op jit(solution)/shard_map/pallas_call | solution.py:309
  9.8 0.0 collective-permute-done.1.near
  9.8 3.4 %collective-permute-done.got = f32[256,256]{1,0:T(8,128)S(1)} collective-permute-done((f32[256,256]{1,0:T(8,128)}, f32[256,256]{1,0:T(8,128)S(1)}, u32[]{:S(2)}, u32[]{:S(2)}) %collective-permute-start) | collective-permute-done | bytes 262176 | tf_op jit(solution)/shard_map/ppermute | solution.py:293
  13.2 1.8 %collective-permute-start.2 = (f32[256,256]{1,0:T(8,128)S(1)}, f32[256,256]{1,0:T(8,128)S(1)}, u32[]{:S(2)}, u32[]{:S(2)}) collective-permute-start(f32[256,256]{1,0:T(8,128)S(1)} %collective-permute-done.got), channel_id=1, source_target_pairs={{0,1},{1,0},{2,3},{3,2},{4,5},{5,4},{6,7},{7,6},{8,9},{9,8},{10,11... | collective-permute-start | bytes 786440 | tf_op jit(solution)/shard_map/ppermute | solution.py:316
  15.0 0.0 collective-permute-start.3
  15.1 1.3 %collective-permute-done.3.near_swapped = f32[128,256]{1,0:T(8,128)S(1)} collective-permute-done((f32[128,256]{1,0:T(8,128)S(1)}, f32[128,256]{1,0:T(8,128)S(1)}, u32[]{:S(2)}, u32[]{:S(2)}) %collective-permute-start.3) | collective-permute-done | bytes 131104 | tf_op jit(solution)/shard_map/ppermute | solution.py:317
  16.4 0.0 collective-permute-done.2.swapped
  16.4 0.0 copy-done.1
  16.4 11.1 %shard_map.48 = (f32[128,256]{1,0:T(8,128)S(1)}, f32[128,256]{1,0:T(8,128)S(1)}) custom-call(f32[4,2,256,256]{3,2,1,0:T(8,128)S(1)} %get-tuple-element.16.mu_in, f32[4,2,256,256]{3,2,1,0:T(8,128)S(1)} %bitcast.8, f32[4,256,128]{2,1,0:T(8,128)S(1)} %get-tuple-element.17.h_same, f32[4,256,128]{2,1,0:T(8,128)S(1)} %get-tuple-element.18.h_cross, ...), custom_call_target="tpu_custom_call" | custom-call | tf_op jit(solution)/shard_map/pallas_call | solution.py:320
  27.5 0.5 collective-permute-start.4
  27.9 1.0 %collective-permute-done.4 = f32[128,256]{1,0:T(8,128)S(1)} collective-permute-done((f32[128,256]{1,0:T(8,128)S(1)}, f32[128,256]{1,0:T(8,128)S(1)}, u32[]{:S(2)}, u32[]{:S(2)}) %collective-permute-start.4) | collective-permute-done | bytes 131104 | tf_op jit(solution)/shard_map/ppermute | solution.py:330
  29.0 1.3 %collective-permute-start.7 = (f32[128,256]{1,0:T(8,128)S(1)}, f32[128,256]{1,0:T(8,128)S(1)}, u32[]{:S(2)}, u32[]{:S(2)}) collective-permute-start(f32[128,256]{1,0:T(8,128)S(1)} %add.33), channel_id=1, source_target_pairs={{0,6},{1,7},{2,4},{3,5},{4,2},{5,3},{6,0},{7,1},{8,14},{9,15},{10,... | collective-permute-start | bytes 393224 | tf_op jit(solution)/shard_map/ppermute | solution.py:344
  30.3 0.0 collective-permute-start.6
  30.3 2.6 %collective-permute-start.5 = (f32[128,256]{1,0:T(8,128)S(1)}, f32[128,256]{1,0:T(8,128)S(1)}, u32[]{:S(2)}, u32[]{:S(2)}) collective-permute-start(f32[128,256]{1,0:T(8,128)S(1)} %add.33), channel_id=1, source_target_pairs={{0,4},{1,5},{2,6},{3,7},{4,0},{5,1},{6,2},{7,3},{8,12},{9,13},{10,... | collective-permute-start | bytes 393224 | tf_op jit(solution)/shard_map/ppermute | solution.py:344
  32.9 2.1 %collective-permute-done.7 = f32[128,256]{1,0:T(8,128)S(1)} collective-permute-done((f32[128,256]{1,0:T(8,128)S(1)}, f32[128,256]{1,0:T(8,128)S(1)}, u32[]{:S(2)}, u32[]{:S(2)}) %collective-permute-start.7) | collective-permute-done | bytes 131104 | tf_op jit(solution)/shard_map/ppermute | solution.py:344
  35.0 0.0 collective-permute-done.6
  35.0 3.7 %collective-permute-done.5 = f32[128,256]{1,0:T(8,128)S(1)} collective-permute-done((f32[128,256]{1,0:T(8,128)S(1)}, f32[128,256]{1,0:T(8,128)S(1)}, u32[]{:S(2)}, u32[]{:S(2)}) %collective-permute-start.5) | collective-permute-done | bytes 131104 | tf_op jit(solution)/shard_map/ppermute | solution.py:344
  38.7 1.6 %collective-permute-start.10 = (f32[128,256]{1,0:T(8,128)S(1)}, f32[128,256]{1,0:T(8,128)S(1)}, u32[]{:S(2)}, u32[]{:S(2)}) collective-permute-start(f32[128,256]{1,0:T(8,128)S(1)} %add_add_fusion.1), channel_id=1, source_target_pairs={{0,24},{1,25},{2,26},{3,27},{4,28},{5,29},{6,30},{7,31},{8,16},{9,... | collective-permute-start | bytes 393224 | tf_op jit(solution)/shard_map/ppermute | solution.py:344
  40.3 0.0 collective-permute-start.9
  40.3 2.4 %collective-permute-start.8 = (f32[128,256]{1,0:T(8,128)S(1)}, f32[128,256]{1,0:T(8,128)S(1)}, u32[]{:S(2)}, u32[]{:S(2)}) collective-permute-start(f32[128,256]{1,0:T(8,128)S(1)} %add_add_fusion.1), channel_id=1, source_target_pairs={{0,16},{1,17},{2,18},{3,19},{4,20},{5,21},{6,22},{7,23},{8,24},{9,... | collective-permute-start | bytes 393224 | tf_op jit(solution)/shard_map/ppermute | solution.py:344
  42.6 1.2 %collective-permute-done.10 = f32[128,256]{1,0:T(8,128)S(1)} collective-permute-done((f32[128,256]{1,0:T(8,128)S(1)}, f32[128,256]{1,0:T(8,128)S(1)}, u32[]{:S(2)}, u32[]{:S(2)}) %collective-permute-start.10) | collective-permute-done | bytes 131104 | tf_op jit(solution)/shard_map/ppermute | solution.py:344
  43.8 0.3 collective-permute-done.9
  44.1 2.8 %collective-permute-done.8 = f32[128,256]{1,0:T(8,128)S(1)} collective-permute-done((f32[128,256]{1,0:T(8,128)S(1)}, f32[128,256]{1,0:T(8,128)S(1)}, u32[]{:S(2)}, u32[]{:S(2)}) %collective-permute-start.8) | collective-permute-done | bytes 131104 | tf_op jit(solution)/shard_map/ppermute | solution.py:344
  46.9 6.8 %collective-permute-start.11 = (f32[128,256]{1,0:T(8,128)S(1)}, f32[128,256]{1,0:T(8,128)S(1)}, u32[]{:S(2)}, u32[]{:S(2)}) collective-permute-start(f32[128,256]{1,0:T(8,128)S(1)} %add_add_fusion), channel_id=1, source_target_pairs={{0,32},{1,33},{2,34},{3,35},{4,36},{5,37},{6,38},{7,39},{8,40},{9,... | collective-permute-start | bytes 393224 | tf_op jit(solution)/shard_map/ppermute | solution.py:344
  53.7 4.2 %collective-permute-done.11 = f32[128,256]{1,0:T(8,128)S(1)} collective-permute-done((f32[128,256]{1,0:T(8,128)S(1)}, f32[128,256]{1,0:T(8,128)S(1)}, u32[]{:S(2)}, u32[]{:S(2)}) %collective-permute-start.11) | collective-permute-done | bytes 131104 | tf_op jit(solution)/shard_map/ppermute | solution.py:344
  58.0 1.7 %collective-permute-start.12 = (f32[128,256]{1,0:T(8,128)S(1)}, f32[128,256]{1,0:T(8,128)S(1)}, u32[]{:S(2)}, u32[]{:S(2)}) collective-permute-start(f32[128,256]{1,0:T(8,128)S(1)} %subtract_maximum_fusion), channel_id=1, source_target_pairs={{0,1},{1,0},{2,3},{3,2},{4,5},{5,4},{6,7},{7,6},{8,9},{9,8},{10,11... | collective-permute-start | bytes 393224 | tf_op jit(solution)/shard_map/ppermute | solution.py:347
  59.7 1.0 %collective-permute-done.12 = f32[128,256]{1,0:T(8,128)S(1)} collective-permute-done((f32[128,256]{1,0:T(8,128)S(1)}, f32[128,256]{1,0:T(8,128)S(1)}, u32[]{:S(2)}, u32[]{:S(2)}) %collective-permute-start.12) | collective-permute-done | bytes 131104 | tf_op jit(solution)/shard_map/ppermute | solution.py:347
  60.7 0.7 %maximum_select_fusion = f32[1,256,256]{2,1,0:T(8,128)} fusion(f32[1,128,256]{2,1,0:T(8,128)S(1)} %bitcast.12, f32[1,128,256]{2,1,0:T(8,128)S(1)} %bitcast.11, pred[]{:T(512)S(6)} %eq.5), kind=kLoop, calls=%fused_computation | loop fusion | flops 196608 | bytes 524289 | tf_op jit(solution)/shard_map/jit(_where)/select_n | solution.py:348
  (4 shorter events, 0.1 us)
Async XLA Ops:
  0.0 4.7 %copy-start.2 = (f32[1,256,256]{2,1,0:T(8,128)S(1)}, f32[1,256,256]{2,1,0:T(8,128)}, u32[]{:S(2)}) copy-start(f32[1,256,256]{2,1,0:T(8,128)} %param.4) | copy-start | bytes 786436
  0.0 4.7 %copy-start = (f32[4,2,256,256]{3,2,1,0:T(8,128)S(1)}, f32[4,2,256,256]{3,2,1,0:T(8,128)}, u32[]{:S(2)}) copy-start(f32[4,2,256,256]{3,2,1,0:T(8,128)} %dual.1) | copy-start | bytes 6291460
  0.0 13.2 %collective-permute-start = (f32[256,256]{1,0:T(8,128)}, f32[256,256]{1,0:T(8,128)S(1)}, u32[]{:S(2)}, u32[]{:S(2)}) collective-permute-start(f32[256,256]{1,0:T(8,128)} %bitcast.9), channel_id=1, source_target_pairs={{192,0},{194,2},{196,4},{198,6},{200,8},{202,10},{204,12},{206,14}... | collective-permute-start | bytes 786440 | tf_op jit(solution)/shard_map/ppermute | solution.py:293
  2.4 7.5 %collective-permute-start.1 = (f32[128,256]{1,0:T(8,128)S(1)}, f32[128,256]{1,0:T(8,128)S(1)}, u32[]{:S(2)}, u32[]{:S(2)}) collective-permute-start(f32[128,256]{1,0:T(8,128)S(1)} %dynamic-slice_bitcast_fusion), channel_id=1, source_target_pairs={{64,0},{66,2},{68,4},{70,6},{72,8},{74,10},{76,12},{78,14},{80,16}... | collective-permute-start | bytes 393224 | tf_op jit(solution)/shard_map/ppermute | solution.py:299
  4.7 1.0 %copy-start.3 = (f32[256,256]{1,0:T(8,128)S(1)}, f32[256,256]{1,0:T(8,128)}, u32[]{:S(2)}) copy-start(f32[256,256]{1,0:T(8,128)} %phase.1) | copy-start | bytes 786436
  5.7 10.7 %copy-start.1 = (f32[1,4,2,256,256]{4,3,2,1,0:T(8,128)S(1)}, f32[1,4,2,256,256]{4,3,2,1,0:T(8,128)}, u32[]{:S(2)}) copy-start(f32[1,4,2,256,256]{4,3,2,1,0:T(8,128)} %param.6) | copy-start | bytes 6291460
  13.2 3.2 %collective-permute-start.2 = (f32[256,256]{1,0:T(8,128)S(1)}, f32[256,256]{1,0:T(8,128)S(1)}, u32[]{:S(2)}, u32[]{:S(2)}) collective-permute-start(f32[256,256]{1,0:T(8,128)S(1)} %collective-permute-done.got), channel_id=1, source_target_pairs={{0,1},{1,0},{2,3},{3,2},{4,5},{5,4},{6,7},{7,6},{8,9},{9,8},{10,11... | collective-permute-start | bytes 786440 | tf_op jit(solution)/shard_map/ppermute | solution.py:316
  15.0 1.3 %collective-permute-start.3 = (f32[128,256]{1,0:T(8,128)S(1)}, f32[128,256]{1,0:T(8,128)S(1)}, u32[]{:S(2)}, u32[]{:S(2)}) collective-permute-start(f32[128,256]{1,0:T(8,128)S(1)} %collective-permute-done.1.near), channel_id=1, source_target_pairs={{0,1},{1,0},{2,3},{3,2},{4,5},{5,4},{6,7},{7,6},{8,9},{9,8},{10,11... | collective-permute-start | bytes 393224 | tf_op jit(solution)/shard_map/ppermute | solution.py:317
  27.5 1.5 %collective-permute-start.4 = (f32[128,256]{1,0:T(8,128)S(1)}, f32[128,256]{1,0:T(8,128)S(1)}, u32[]{:S(2)}, u32[]{:S(2)}) collective-permute-start(f32[128,256]{1,0:T(8,128)S(1)} %get-tuple-element.24), channel_id=1, source_target_pairs={{0,1},{1,0},{2,3},{3,2},{4,5},{5,4},{6,7},{7,6},{8,9},{9,8},{10,11... | collective-permute-start | bytes 393224 | tf_op jit(solution)/shard_map/ppermute | solution.py:330
  29.0 6.0 %collective-permute-start.7 = (f32[128,256]{1,0:T(8,128)S(1)}, f32[128,256]{1,0:T(8,128)S(1)}, u32[]{:S(2)}, u32[]{:S(2)}) collective-permute-start(f32[128,256]{1,0:T(8,128)S(1)} %add.33), channel_id=1, source_target_pairs={{0,6},{1,7},{2,4},{3,5},{4,2},{5,3},{6,0},{7,1},{8,14},{9,15},{10,... | collective-permute-start | bytes 393224 | tf_op jit(solution)/shard_map/ppermute | solution.py:344
  30.3 4.7 %collective-permute-start.6 = (f32[128,256]{1,0:T(8,128)S(1)}, f32[128,256]{1,0:T(8,128)S(1)}, u32[]{:S(2)}, u32[]{:S(2)}) collective-permute-start(f32[128,256]{1,0:T(8,128)S(1)} %add.33), channel_id=1, source_target_pairs={{0,2},{1,3},{2,0},{3,1},{4,6},{5,7},{6,4},{7,5},{8,10},{9,11},{10,... | collective-permute-start | bytes 393224 | tf_op jit(solution)/shard_map/ppermute | solution.py:344
  30.3 8.4 %collective-permute-start.5 = (f32[128,256]{1,0:T(8,128)S(1)}, f32[128,256]{1,0:T(8,128)S(1)}, u32[]{:S(2)}, u32[]{:S(2)}) collective-permute-start(f32[128,256]{1,0:T(8,128)S(1)} %add.33), channel_id=1, source_target_pairs={{0,4},{1,5},{2,6},{3,7},{4,0},{5,1},{6,2},{7,3},{8,12},{9,13},{10,... | collective-permute-start | bytes 393224 | tf_op jit(solution)/shard_map/ppermute | solution.py:344
  38.7 5.1 %collective-permute-start.10 = (f32[128,256]{1,0:T(8,128)S(1)}, f32[128,256]{1,0:T(8,128)S(1)}, u32[]{:S(2)}, u32[]{:S(2)}) collective-permute-start(f32[128,256]{1,0:T(8,128)S(1)} %add_add_fusion.1), channel_id=1, source_target_pairs={{0,24},{1,25},{2,26},{3,27},{4,28},{5,29},{6,30},{7,31},{8,16},{9,... | collective-permute-start | bytes 393224 | tf_op jit(solution)/shard_map/ppermute | solution.py:344
  40.3 3.8 %collective-permute-start.9 = (f32[128,256]{1,0:T(8,128)S(1)}, f32[128,256]{1,0:T(8,128)S(1)}, u32[]{:S(2)}, u32[]{:S(2)}) collective-permute-start(f32[128,256]{1,0:T(8,128)S(1)} %add_add_fusion.1), channel_id=1, source_target_pairs={{0,8},{1,9},{2,10},{3,11},{4,12},{5,13},{6,14},{7,15},{8,0},{9,1},... | collective-permute-start | bytes 393224 | tf_op jit(solution)/shard_map/ppermute | solution.py:344
  40.3 6.6 %collective-permute-start.8 = (f32[128,256]{1,0:T(8,128)S(1)}, f32[128,256]{1,0:T(8,128)S(1)}, u32[]{:S(2)}, u32[]{:S(2)}) collective-permute-start(f32[128,256]{1,0:T(8,128)S(1)} %add_add_fusion.1), channel_id=1, source_target_pairs={{0,16},{1,17},{2,18},{3,19},{4,20},{5,21},{6,22},{7,23},{8,24},{9,... | collective-permute-start | bytes 393224 | tf_op jit(solution)/shard_map/ppermute | solution.py:344
  46.9 11.0 %collective-permute-start.11 = (f32[128,256]{1,0:T(8,128)S(1)}, f32[128,256]{1,0:T(8,128)S(1)}, u32[]{:S(2)}, u32[]{:S(2)}) collective-permute-start(f32[128,256]{1,0:T(8,128)S(1)} %add_add_fusion), channel_id=1, source_target_pairs={{0,32},{1,33},{2,34},{3,35},{4,36},{5,37},{6,38},{7,39},{8,40},{9,... | collective-permute-start | bytes 393224 | tf_op jit(solution)/shard_map/ppermute | solution.py:344
  58.0 2.7 %collective-permute-start.12 = (f32[128,256]{1,0:T(8,128)S(1)}, f32[128,256]{1,0:T(8,128)S(1)}, u32[]{:S(2)}, u32[]{:S(2)}) collective-permute-start(f32[128,256]{1,0:T(8,128)S(1)} %subtract_maximum_fusion), channel_id=1, source_target_pairs={{0,1},{1,0},{2,3},{3,2},{4,5},{5,4},{6,7},{7,6},{8,9},{9,8},{10,11... | collective-permute-start | bytes 393224 | tf_op jit(solution)/shard_map/ppermute | solution.py:347
